TPU v7x, 512 devices: a whole 4x4x16 slice. The times are simulated.
512 devices in a mesh: gz: 8 (over z_lo), xy: 64 (over y, z_hi, x, core).
Axes of the slice: x: 4, y: 4, z: 16 (z_hi: 2, z_lo: 8; z = z_hi * 8 + z_lo), core: 2. Of those that a mesh axis runs over, the one named last changes fastest.
Arguments:
- populations: float32 [19, 512, 64, 128], P(None, 'xy', 'gz'), may hold values from 0.02 to 0.08
- colour: float32 [512, 64, 128], P('xy', 'gz'), may hold values from -1 to 1
- conformation: float32 [6, 512, 64, 128], P(None, 'xy', 'gz'), may hold values from -1.5 to 1.5
- labels: int32 [512, 64, 128], P('xy', 'gz'), may hold values from 0 to 2
- pop_cotangent: float32 [19, 512, 64, 128], P(None, 'xy', 'gz'), may hold values from -6 to 6
- conf_cotangent: float32 [6, 512, 64, 128], P(None, 'xy', 'gz'), may hold values from -6 to 6
Outputs:
- adj_populations: float32 [19, 512, 64, 128], P(None, 'xy', 'gz')
- adj_colour: float32 [512, 64, 128], P('xy', 'gz')
- adj_conformation: float32 [6, 512, 64, 128], P(None, 'xy', 'gz')
Inputs may be any that keep to these rules, and one draw needn't show every extreme that they name: `labels`: 0 marks a fluid cell, 1 a solid cell, 2 an inlet cell.
All inputs are finite; a program needn't handle non-finite values.
Results may differ from a plain program's by a relative error of at most 0.0003.
Values sent between devices are 32-bit elements; how exact they have to be, the bound alone decides.
A program may use at most 64 MiB of HBM per device.

v0:
```python
import jax
import jax.numpy as jnp
from jax import lax
from jax.sharding import PartitionSpec as P

velocities = (
    (0, 0, 0),
    (1, 0, 0),
    (-1, 0, 0),
    (0, 1, 0),
    (0, -1, 0),
    (0, 0, 1),
    (0, 0, -1),
    (1, 1, 0),
    (-1, -1, 0),
    (1, -1, 0),
    (-1, 1, 0),
    (1, 0, 1),
    (-1, 0, -1),
    (1, 0, -1),
    (-1, 0, 1),
    (0, 1, 1),
    (0, -1, -1),
    (0, 1, -1),
    (0, -1, 1),
)
opposite = (0, 2, 1, 4, 3, 6, 5, 8, 7, 10, 9, 12, 11, 14, 13, 16, 15, 18, 17)
lattice_weights = (1.0 / 3.0,) + (1.0 / 18.0,) * 6 + (1.0 / 36.0,) * 12
component_slot = {
    (0, 0): 0,
    (1, 1): 1,
    (2, 2): 2,
    (0, 1): 3,
    (1, 0): 3,
    (0, 2): 4,
    (2, 0): 4,
    (1, 2): 5,
    (2, 1): 5,
}
relax_time = 0.8
time_step = 0.5
relax_rate = 0.1
smooth_speed = 0.02
inlet_speed = 0.05


def extended(cells, sides, width):
    for axis, dim in sides:
        count = lax.axis_size(axis)
        head = lax.slice_in_dim(cells, 0, width, axis=dim)
        tail = lax.slice_in_dim(cells, cells.shape[dim] - width, cells.shape[dim], axis=dim)
        cells = jnp.concatenate(
            [
                lax.ppermute(tail, axis, [(i, (i + 1) % count) for i in range(count)]),
                cells,
                lax.ppermute(head, axis, [((i + 1) % count, i) for i in range(count)]),
            ],
            axis=dim,
        )
    return cells


def shifted_2(block, axis, distance):
    devices = range(lax.axis_size(axis))
    route = [((i - distance) % len(devices), i) for i in devices]
    return lax.ppermute(block, axis, route)


def axis_derivative(padded, which):
    if which == 0:
        return 0.5 * (padded[:, 2:, 1:-1, :] - padded[:, :-2, 1:-1, :])
    if which == 2:
        return 0.5 * (padded[:, 1:-1, 2:, :] - padded[:, 1:-1, :-2, :])
    middle = padded[:, 1:-1, 1:-1, :]
    return 0.5 * (jnp.roll(middle, -1, axis=3) - jnp.roll(middle, 1, axis=3))


def axis_curvature(padded, which):
    middle = padded[:, 1:-1, 1:-1, :]
    if which == 0:
        return padded[:, 2:, 1:-1, :] + padded[:, :-2, 1:-1, :] - 2.0 * middle
    if which == 2:
        return padded[:, 1:-1, 2:, :] + padded[:, 1:-1, :-2, :] - 2.0 * middle
    return jnp.roll(middle, -1, axis=3) + jnp.roll(middle, 1, axis=3) - 2.0 * middle


def equilibrium(density, flow):
    square = flow[0] * flow[0] + flow[1] * flow[1] + flow[2] * flow[2]
    result = []
    for direction in range(19):
        vector = velocities[direction]
        along = vector[0] * flow[0] + vector[1] * flow[1] + vector[2] * flow[2]
        result.append(
            lattice_weights[direction]
            * density
            * (1.0 + 3.0 * along + 4.5 * along * along - 1.5 * square)
        )
    return jnp.stack(result)


def local_step(populations, labels, colour_padded, conform_padded):
    density = jnp.sum(populations, axis=0)
    velocity = []
    for which in range(3):
        moment = jnp.zeros_like(density)
        for direction in range(19):
            if velocities[direction][which] != 0:
                moment = moment + velocities[direction][which] * populations[direction]
        velocity.append(moment / density)
    phase = colour_padded[0, 1:-1, 1:-1, :]
    stress = []
    for slot_a in range(3):
        for slot_b in range(3):
            if slot_b >= slot_a:
                total = conform_padded[component_slot[slot_a, slot_b]]
                for middle in range(3):
                    total = (
                        total
                        + 0.5
                        * conform_padded[component_slot[slot_a, middle]]
                        * conform_padded[component_slot[middle, slot_b]]
                    )
                stress.append(total)
    stress = jnp.stack(stress)
    stress_slot = {(0, 0): 0, (0, 1): 1, (0, 2): 2, (1, 1): 3, (1, 2): 4, (2, 2): 5}
    force = []
    for slot_a in range(3):
        total = (1.0 - phase * phase) * axis_derivative(colour_padded, slot_a)[0]
        for slot_b in range(3):
            index = stress_slot[min(slot_a, slot_b), max(slot_a, slot_b)]
            total = total + axis_derivative(stress[index : index + 1], slot_b)[0]
        force.append(total)
    shifted = [velocity[k] + force[k] / (2.0 * density) for k in range(3)]
    balance = equilibrium(density, shifted)
    shift_force = shifted[0] * force[0] + shifted[1] * force[1] + shifted[2] * force[2]
    factor = 1.0 - 0.5 / relax_time
    sources = []
    for direction in range(19):
        vector = velocities[direction]
        along_force = vector[0] * force[0] + vector[1] * force[1] + vector[2] * force[2]
        along_flow = vector[0] * shifted[0] + vector[1] * shifted[1] + vector[2] * shifted[2]
        sources.append(
            factor
            * lattice_weights[direction]
            * (3.0 * (along_force - shift_force) + 9.0 * along_flow * along_force)
        )
    collided = populations - (populations - balance) / relax_time + jnp.stack(sources)
    zeros_field = jnp.zeros_like(density)
    inlet = equilibrium(density, [zeros_field, zeros_field, zeros_field + inlet_speed])
    bounced = jnp.stack([populations[k] for k in opposite])
    marks = labels[None]
    post = jnp.where(marks == 1, bounced, jnp.where(marks == 2, inlet, collided))
    conform_centre = conform_padded[:, 1:-1, 1:-1, :]
    advection = jnp.zeros_like(conform_centre)
    for which in range(3):
        speed = jnp.sqrt(velocity[which] * velocity[which] + smooth_speed * smooth_speed)
        advection = (
            advection
            + velocity[which][None] * axis_derivative(conform_padded, which)
            - 0.5 * speed[None] * axis_curvature(conform_padded, which)
        )
    conform_next = conform_centre - time_step * advection - relax_rate * conform_centre
    return (post, conform_next)


def body(populations, colour, conformation, labels, pop_cotangent, conf_cotangent):
    count_x = populations.shape[1]
    count_z = populations.shape[2]
    fields = jnp.concatenate([colour[None], conformation], axis=0)
    field_pad = extended(fields, (("gz", 2), ("xy", 1)), 1)
    pop_pad = extended(pop_cotangent, (("gz", 2), ("xy", 1)), 1)
    adj_post = []
    for direction in range(19):
        vector = velocities[direction]
        window = pop_pad[
            direction,
            1 + vector[0] : 1 + vector[0] + count_x,
            1 + vector[2] : 1 + vector[2] + count_z,
            :,
        ]
        adj_post.append(jnp.roll(window, -vector[1], axis=2))
    adj_post = jnp.stack(adj_post)

    def step_local(pop_values, colour_padded, conform_padded):
        return local_step(pop_values, labels, colour_padded, conform_padded)

    outputs, pullback = jax.vjp(step_local, populations, field_pad[:1], field_pad[1:])
    adj_populations, adj_colour_pad, adj_conf_pad = pullback((adj_post, conf_cotangent))
    adj_fields = jnp.concatenate([adj_colour_pad, adj_conf_pad], axis=0)
    interior = adj_fields[:, 1:-1, 1:-1, :]
    from_next = shifted_2(adj_fields[:, 0, 1:-1, :], "xy", -1)
    from_prior = shifted_2(adj_fields[:, count_x + 1, 1:-1, :], "xy", 1)
    interior = interior.at[:, count_x - 1, :, :].add(from_next)
    interior = interior.at[:, 0, :, :].add(from_prior)
    from_upper = shifted_2(adj_fields[:, 1:-1, 0, :], "gz", -1)
    from_lower = shifted_2(adj_fields[:, 1:-1, count_z + 1, :], "gz", 1)
    interior = interior.at[:, :, count_z - 1, :].add(from_upper)
    interior = interior.at[:, :, 0, :].add(from_lower)
    return (adj_populations, interior[0], interior[1:])


def solution(mesh):
    placed = (
        P(None, "xy", "gz", None),
        P("xy", "gz", None),
        P(None, "xy", "gz", None),
        P("xy", "gz", None),
        P(None, "xy", "gz", None),
        P(None, "xy", "gz", None),
    )
    return jax.shard_map(
        body,
        mesh=mesh,
        in_specs=placed,
        out_specs=(P(None, "xy", "gz", None), P("xy", "gz", None), P(None, "xy", "gz", None)),
        check_vma=False,
    )
```

profile of v0, /device:TPU:32, one launch (start us, length us, event | category | flops | bytes accessed | tf_op | source)
XLA Modules:
  0.0 125.3 jit_solution(12080360125291174813)
XLA Ops:
  0.6 1.1 pad_maximum_fusion.31
  1.8 7.4 %collective-permute-start.4 = (f32[7,8,1,128]{3,1,2,0:T(8,128)S(1)}, f32[7,8,1,128]{3,1,2,0:T(8,128)S(1)}, u32[]{:S(2)}, u32[]{:S(2)}) collective-permute-start(f32[7,8,1,128]{3,1,2,0:T(8,128)S(1)} %bitcast.834), channel_id=1, source_target_pairs={{64,0},{128,64},{192,128},{256,192},{320,256},{384,320},{448,384},... | collective-permute-start | bytes 86024 | tf_op jit(solution)/shard_map/ppermute | solution.py:56
  9.2 1.9 %collective-permute-start.5 = (f32[7,8,1,128]{3,1,2,0:T(8,128)S(1)}, f32[7,8,1,128]{3,1,2,0:T(8,128)S(1)}, u32[]{:S(2)}, u32[]{:S(2)}) collective-permute-start(f32[7,8,1,128]{3,1,2,0:T(8,128)S(1)} %bitcast.833), channel_id=1, source_target_pairs={{0,64},{64,128},{128,192},{192,256},{256,320},{320,384},{384,448},... | collective-permute-start | bytes 86024 | tf_op jit(solution)/shard_map/ppermute | solution.py:54
  11.1 1.5 %fusion.394 = (f32[19,8,1,128]{3,2,1,0:T(1,128)S(1)}, f32[19,8,1,128]{3,2,1,0:T(1,128)S(1)}) fusion(f32[19,8,8,128]{3,2,1,0:T(8,128)} %param.18), kind=kLoop, calls=%fused_computation.935 | loop fusion | bytes 311296 | tf_op jit(solution)/shard_map/slice | solution.py:50
  12.6 1.9 %collective-permute-start = (f32[19,8,1,128]{3,1,2,0:T(8,128)S(1)}, f32[19,8,1,128]{3,1,2,0:T(8,128)S(1)}, u32[]{:S(2)}, u32[]{:S(2)}) collective-permute-start(f32[19,8,1,128]{3,1,2,0:T(8,128)S(1)} %copy.392), channel_id=1, source_target_pairs={{0,64},{64,128},{128,192},{192,256},{256,320},{320,384},{384,448},... | collective-permute-start | bytes 233480 | tf_op jit(solution)/shard_map/ppermute | solution.py:54
  14.6 7.9 %collective-permute-start.1 = (f32[19,8,1,128]{3,1,2,0:T(8,128)S(1)}, f32[19,8,1,128]{3,1,2,0:T(8,128)S(1)}, u32[]{:S(2)}, u32[]{:S(2)}) collective-permute-start(f32[19,8,1,128]{3,1,2,0:T(8,128)S(1)} %copy.393), channel_id=1, source_target_pairs={{64,0},{128,64},{192,128},{256,192},{320,256},{384,320},{448,384},... | collective-permute-start | bytes 233480 | tf_op jit(solution)/shard_map/ppermute | solution.py:56
  23.0 0.1 fusion.397
  23.1 0.6 copy-done.4
  23.8 1.9 %collective-permute-start.7 = (f32[7,1,10,128]{3,2,1,0:T(8,128)S(1)}, f32[7,1,10,128]{3,2,1,0:T(8,128)S(1)}, u32[]{:S(2)}, u32[]{:S(2)}) collective-permute-start(f32[7,1,10,128]{3,2,1,0:T(8,128)S(1)} %get-tuple-element.305), channel_id=1, source_target_pairs={{0,1},{1,2},{2,3},{3,4},{4,5},{5,6},{6,7},{7,8},{8,9},{9,10},{10,1... | collective-permute-start | bytes 107528 | tf_op jit(solution)/shard_map/ppermute | solution.py:54
  25.7 16.6 %collective-permute-start.6 = (f32[7,1,10,128]{3,2,1,0:T(8,128)S(1)}, f32[7,1,10,128]{3,2,1,0:T(8,128)S(1)}, u32[]{:S(2)}, u32[]{:S(2)}) collective-permute-start(f32[7,1,10,128]{3,2,1,0:T(8,128)S(1)} %get-tuple-element.306), channel_id=1, source_target_pairs={{1,0},{2,1},{3,2},{4,3},{5,4},{6,5},{7,6},{8,7},{9,8},{10,9},{11,1... | collective-permute-start | bytes 107528 | tf_op jit(solution)/shard_map/ppermute | solution.py:56
  42.5 1.6 %collective-permute-done.6 = f32[7,1,10,128]{3,2,1,0:T(8,128)S(1)} collective-permute-done((f32[7,1,10,128]{3,2,1,0:T(8,128)S(1)}, f32[7,1,10,128]{3,2,1,0:T(8,128)S(1)}, u32[]{:S(2)}, u32[]{:S(2)}) %collective-permute-start.6) | collective-permute-done | bytes 35872 | tf_op jit(solution)/shard_map/ppermute | solution.py:56
  44.7 0.2 multiply_add_fusion.75
  45.0 0.6 copy-done.3
  45.6 0.2 multiply_reduce_fusion.4
  45.8 0.2 multiply_reduce_fusion.2
  46.1 0.2 constant_dynamic-update-slice_fusion.5
  46.3 0.1 fusion.392
  46.5 1.9 %collective-permute-start.3 = (f32[19,1,10,128]{3,1,2,0:T(1,128)S(1)}, f32[19,1,10,128]{3,1,2,0:T(1,128)S(1)}, u32[]{:S(2)}, u32[]{:S(2)}) collective-permute-start(f32[19,1,10,128]{3,1,2,0:T(1,128)S(1)} %get-tuple-element.202), channel_id=1, source_target_pairs={{0,1},{1,2},{2,3},{3,4},{4,5},{5,6},{6,7},{7,8},{8,9},{9,10},{10,1... | collective-permute-start | bytes 291848 | tf_op jit(solution)/shard_map/ppermute | solution.py:54
  48.8 16.6 %collective-permute-start.2 = (f32[19,1,10,128]{3,1,2,0:T(1,128)S(1)}, f32[19,1,10,128]{3,1,2,0:T(1,128)S(1)}, u32[]{:S(2)}, u32[]{:S(2)}) collective-permute-start(f32[19,1,10,128]{3,1,2,0:T(1,128)S(1)} %get-tuple-element.203), channel_id=1, source_target_pairs={{1,0},{2,1},{3,2},{4,3},{5,4},{6,5},{7,6},{8,7},{9,8},{10,9},{11,1... | collective-permute-start | bytes 291848 | tf_op jit(solution)/shard_map/ppermute | solution.py:56
  65.5 0.2 collective-permute-done.3
  65.7 0.3 copy_dynamic-update-slice_fusion
  66.0 0.1 fusion.390
  66.3 1.6 %collective-permute-done.2 = f32[19,1,10,128]{3,1,2,0:T(1,128)S(1)} collective-permute-done((f32[19,1,10,128]{3,1,2,0:T(1,128)S(1)}, f32[19,1,10,128]{3,1,2,0:T(1,128)S(1)}, u32[]{:S(2)}, u32[]{:S(2)}) %collective-permute-start.2) | collective-permute-done | bytes 97312 | tf_op jit(solution)/shard_map/ppermute | solution.py:56
  67.9 0.1 fusion.391
  69.1 0.3 fusion
  69.4 0.7 fusion.371
  70.1 0.2 fusion.373
  70.3 0.2 fusion.375
  71.6 0.1 multiply_multiply_fusion.3
  71.7 0.1 multiply_multiply_fusion.20
  71.9 0.2 negate_multiply_fusion.2
  72.3 0.1 fusion.395
  72.6 0.1 split.112
  72.9 0.2 add_add_fusion.1
  73.1 0.2 add_add_fusion.2
  73.3 0.2 copy-done.7
  73.6 1.1 select_add_fusion
  74.8 16.8 %collective-permute-start.8 = (f32[7,8,128]{2,1,0:T(8,128)S(1)}, f32[7,8,128]{2,1,0:T(8,128)S(1)}, u32[]{:S(2)}, u32[]{:S(2)}) collective-permute-start(f32[7,8,128]{2,1,0:T(8,128)S(1)} %fusion.367), channel_id=1, source_target_pairs={{1,0},{2,1},{3,2},{4,3},{5,4},{6,5},{7,6},{8,7},{9,8},{10,9},{11,1... | collective-permute-start | bytes 86024 | tf_op jit(solution)/shard_map/ppermute | solution.py:66
  91.7 10.1 %collective-permute-start.10 = (f32[7,8,128]{2,1,0:T(8,128)S(1)}, f32[7,8,128]{2,1,0:T(8,128)S(1)}, u32[]{:S(2)}, u32[]{:S(2)}) collective-permute-start(f32[7,8,128]{2,1,0:T(8,128)S(1)} %bitcast.836), channel_id=1, source_target_pairs={{64,0},{128,64},{192,128},{256,192},{320,256},{384,320},{448,384},... | collective-permute-start | bytes 86024 | tf_op jit(solution)/shard_map/ppermute | solution.py:66
  101.8 1.9 %collective-permute-start.11 = (f32[7,8,128]{2,1,0:T(8,128)S(1)}, f32[7,8,128]{2,1,0:T(8,128)S(1)}, u32[]{:S(2)}, u32[]{:S(2)}) collective-permute-start(f32[7,8,128]{2,1,0:T(8,128)S(1)} %bitcast.835), channel_id=1, source_target_pairs={{448,0},{0,64},{64,128},{128,192},{192,256},{256,320},{320,384},{3... | collective-permute-start | bytes 86024 | tf_op jit(solution)/shard_map/ppermute | solution.py:66
  103.7 1.7 %fusion.166 = f32[8,8,128]{2,1,0:T(8,128)S(1)} fusion(f32[8,8,128]{2,1,0:T(8,128)S(1)} %get-tuple-element.72, f32[8,8,128]{2,1,0:T(8,128)S(1)} %get-tuple-element.70, f32[8,8,128]{2,1,0:T(8,128)S(1)} %get-tuple-element.303, f32[1,8,8,128]{3,2,1,0:T(8,128)S(1)} %get-tuple-element.160, f32[8,8,128]{2,1,0:T(8,128)S(1)} %reduce_sum.65, ...), kind=kLoop, calls=%fused_computation.369 | loop fusion | flops 6660096 | bytes 3047424 | tf_op jit(solution)/shard_map/transpose(jvp())/add_any | solution.py:109
  105.5 1.9 %collective-permute-start.9 = (f32[7,8,128]{2,1,0:T(8,128)S(1)}, f32[7,8,128]{2,1,0:T(8,128)S(1)}, u32[]{:S(2)}, u32[]{:S(2)}) collective-permute-start(f32[7,8,128]{2,1,0:T(8,128)S(1)} %get-tuple-element.240), channel_id=1, source_target_pairs={{63,0},{0,1},{1,2},{2,3},{3,4},{4,5},{5,6},{6,7},{7,8},{8,9},{9,10... | collective-permute-start | bytes 86024 | tf_op jit(solution)/shard_map/ppermute | solution.py:66
  107.4 1.1 add_add_fusion
  108.5 15.1 %collective-permute-done.9 = f32[7,8,128]{2,1,0:T(8,128)S(1)} collective-permute-done((f32[7,8,128]{2,1,0:T(8,128)S(1)}, f32[7,8,128]{2,1,0:T(8,128)S(1)}, u32[]{:S(2)}, u32[]{:S(2)}) %collective-permute-start.9) | collective-permute-done | bytes 28704 | tf_op jit(solution)/shard_map/ppermute | solution.py:66
  123.7 0.1 scatter-add.16
  123.8 0.1 scatter-add.19
  124.0 0.6 slice_bitcast_fusion
  124.6 0.7 slice.818
  (115 shorter events, 4.7 us)
Async XLA Ops:
  0.6 21.9 %copy-start.2 = (f32[19,8,8,128]{3,2,1,0:T(8,128)S(1)}, f32[19,8,8,128]{3,2,1,0:T(8,128)}, u32[]{:S(2)}) copy-start(f32[19,8,8,128]{3,2,1,0:T(8,128)} %param.14) | copy-start | bytes 1867780
  1.8 22.0 %collective-permute-start.4 = (f32[7,8,1,128]{3,1,2,0:T(8,128)S(1)}, f32[7,8,1,128]{3,1,2,0:T(8,128)S(1)}, u32[]{:S(2)}, u32[]{:S(2)}) collective-permute-start(f32[7,8,1,128]{3,1,2,0:T(8,128)S(1)} %bitcast.834), channel_id=1, source_target_pairs={{64,0},{128,64},{192,128},{256,192},{320,256},{384,320},{448,384},... | collective-permute-start | bytes 86024 | tf_op jit(solution)/shard_map/ppermute | solution.py:56
  9.2 14.6 %collective-permute-start.5 = (f32[7,8,1,128]{3,1,2,0:T(8,128)S(1)}, f32[7,8,1,128]{3,1,2,0:T(8,128)S(1)}, u32[]{:S(2)}, u32[]{:S(2)}) collective-permute-start(f32[7,8,1,128]{3,1,2,0:T(8,128)S(1)} %bitcast.833), channel_id=1, source_target_pairs={{0,64},{64,128},{128,192},{192,256},{256,320},{320,384},{384,448},... | collective-permute-start | bytes 86024 | tf_op jit(solution)/shard_map/ppermute | solution.py:54
  12.6 10.1 %copy-start.1 = (f32[8,8,128]{2,1,0:T(8,128)S(1)}, f32[8,8,128]{2,1,0:T(8,128)}, u32[]{:S(2)}) copy-start(f32[8,8,128]{2,1,0:T(8,128)} %param.15) | copy-start | bytes 98308
  12.6 33.5 %collective-permute-start = (f32[19,8,1,128]{3,1,2,0:T(8,128)S(1)}, f32[19,8,1,128]{3,1,2,0:T(8,128)S(1)}, u32[]{:S(2)}, u32[]{:S(2)}) collective-permute-start(f32[19,8,1,128]{3,1,2,0:T(8,128)S(1)} %copy.392), channel_id=1, source_target_pairs={{0,64},{64,128},{128,192},{192,256},{256,320},{320,384},{384,448},... | collective-permute-start | bytes 233480 | tf_op jit(solution)/shard_map/ppermute | solution.py:54
  14.6 8.3 %copy-start = (f32[6,8,8,128]{3,2,1,0:T(8,128)S(1)}, f32[6,8,8,128]{3,2,1,0:T(8,128)}, u32[]{:S(2)}) copy-start(f32[6,8,8,128]{3,2,1,0:T(8,128)} %param.16) | copy-start | bytes 589828
  14.6 31.7 %collective-permute-start.1 = (f32[19,8,1,128]{3,1,2,0:T(8,128)S(1)}, f32[19,8,1,128]{3,1,2,0:T(8,128)S(1)}, u32[]{:S(2)}, u32[]{:S(2)}) collective-permute-start(f32[19,8,1,128]{3,1,2,0:T(8,128)S(1)} %copy.393), channel_id=1, source_target_pairs={{64,0},{128,64},{192,128},{256,192},{320,256},{384,320},{448,384},... | collective-permute-start | bytes 233480 | tf_op jit(solution)/shard_map/ppermute | solution.py:56
  22.7 1.1 copy-start.4
  22.9 19.4 %copy-start.5 = (s32[8,8,128]{2,1,0:T(8,128)S(1)}, s32[8,8,128]{2,1,0:T(8,128)}, u32[]{:S(2)}) copy-start(s32[8,8,128]{2,1,0:T(8,128)} %param.17) | copy-start | bytes 98308
  23.8 18.7 %collective-permute-start.7 = (f32[7,1,10,128]{3,2,1,0:T(8,128)S(1)}, f32[7,1,10,128]{3,2,1,0:T(8,128)S(1)}, u32[]{:S(2)}, u32[]{:S(2)}) collective-permute-start(f32[7,1,10,128]{3,2,1,0:T(8,128)S(1)} %get-tuple-element.305), channel_id=1, source_target_pairs={{0,1},{1,2},{2,3},{3,4},{4,5},{5,6},{6,7},{7,8},{8,9},{9,10},{10,1... | collective-permute-start | bytes 107528 | tf_op jit(solution)/shard_map/ppermute | solution.py:54
  25.7 18.4 %collective-permute-start.6 = (f32[7,1,10,128]{3,2,1,0:T(8,128)S(1)}, f32[7,1,10,128]{3,2,1,0:T(8,128)S(1)}, u32[]{:S(2)}, u32[]{:S(2)}) collective-permute-start(f32[7,1,10,128]{3,2,1,0:T(8,128)S(1)} %get-tuple-element.306), channel_id=1, source_target_pairs={{1,0},{2,1},{3,2},{4,3},{5,4},{6,5},{7,6},{8,7},{9,8},{10,9},{11,1... | collective-permute-start | bytes 107528 | tf_op jit(solution)/shard_map/ppermute | solution.py:56
  44.7 0.9 copy-start.3
  46.5 19.2 %collective-permute-start.3 = (f32[19,1,10,128]{3,1,2,0:T(1,128)S(1)}, f32[19,1,10,128]{3,1,2,0:T(1,128)S(1)}, u32[]{:S(2)}, u32[]{:S(2)}) collective-permute-start(f32[19,1,10,128]{3,1,2,0:T(1,128)S(1)} %get-tuple-element.202), channel_id=1, source_target_pairs={{0,1},{1,2},{2,3},{3,4},{4,5},{5,6},{6,7},{7,8},{8,9},{9,10},{10,1... | collective-permute-start | bytes 291848 | tf_op jit(solution)/shard_map/ppermute | solution.py:54
  48.8 19.1 %collective-permute-start.2 = (f32[19,1,10,128]{3,1,2,0:T(1,128)S(1)}, f32[19,1,10,128]{3,1,2,0:T(1,128)S(1)}, u32[]{:S(2)}, u32[]{:S(2)}) collective-permute-start(f32[19,1,10,128]{3,1,2,0:T(1,128)S(1)} %get-tuple-element.203), channel_id=1, source_target_pairs={{1,0},{2,1},{3,2},{4,3},{5,4},{6,5},{7,6},{8,7},{9,8},{10,9},{11,1... | collective-permute-start | bytes 291848 | tf_op jit(solution)/shard_map/ppermute | solution.py:56
  72.9 0.7 copy-start.7
  74.8 30.6 %collective-permute-start.8 = (f32[7,8,128]{2,1,0:T(8,128)S(1)}, f32[7,8,128]{2,1,0:T(8,128)S(1)}, u32[]{:S(2)}, u32[]{:S(2)}) collective-permute-start(f32[7,8,128]{2,1,0:T(8,128)S(1)} %fusion.367), channel_id=1, source_target_pairs={{1,0},{2,1},{3,2},{4,3},{5,4},{6,5},{7,6},{8,7},{9,8},{10,9},{11,1... | collective-permute-start | bytes 86024 | tf_op jit(solution)/shard_map/ppermute | solution.py:66
  91.7 31.9 %collective-permute-start.10 = (f32[7,8,128]{2,1,0:T(8,128)S(1)}, f32[7,8,128]{2,1,0:T(8,128)S(1)}, u32[]{:S(2)}, u32[]{:S(2)}) collective-permute-start(f32[7,8,128]{2,1,0:T(8,128)S(1)} %bitcast.836), channel_id=1, source_target_pairs={{64,0},{128,64},{192,128},{256,192},{320,256},{384,320},{448,384},... | collective-permute-start | bytes 86024 | tf_op jit(solution)/shard_map/ppermute | solution.py:66
  101.8 22.0 %collective-permute-start.11 = (f32[7,8,128]{2,1,0:T(8,128)S(1)}, f32[7,8,128]{2,1,0:T(8,128)S(1)}, u32[]{:S(2)}, u32[]{:S(2)}) collective-permute-start(f32[7,8,128]{2,1,0:T(8,128)S(1)} %bitcast.835), channel_id=1, source_target_pairs={{448,0},{0,64},{64,128},{128,192},{192,256},{256,320},{320,384},{3... | collective-permute-start | bytes 86024 | tf_op jit(solution)/shard_map/ppermute | solution.py:66
  105.4 2.0 %copy-start.6 = (pred[19]{0:T(512)(128)(4,1)S(1)}, pred[19]{0:T(512)(128)(4,1)}, u32[]{:S(2)}) copy-start(pred[19]{0:T(512)(128)(4,1)} %constant.225.clone.1) | copy-start | bytes 61
  105.5 18.1 %collective-permute-start.9 = (f32[7,8,128]{2,1,0:T(8,128)S(1)}, f32[7,8,128]{2,1,0:T(8,128)S(1)}, u32[]{:S(2)}, u32[]{:S(2)}) collective-permute-start(f32[7,8,128]{2,1,0:T(8,128)S(1)} %get-tuple-element.240), channel_id=1, source_target_pairs={{63,0},{0,1},{1,2},{2,3},{3,4},{4,5},{5,6},{6,7},{7,8},{8,9},{9,10... | collective-permute-start | bytes 86024 | tf_op jit(solution)/shard_map/ppermute | solution.py:66
where the time goes:
time: 126 us; the launch traced here: 125 us
  starting transfers between devices  87 us (69%)
  waiting for transfers between devices  18.6 us (15%)
  other arithmetic  10.1 us (8%)
  local copies, waits for them, and re-layouts  8.14 us (6%)
  between operations  1.43 us (1%)
    ppermute x4, starting transfers between devices, extended(): lax.ppermute(head, axis, [((i + 1) % count, i) for i in range(count)])  48.5 us
    ppermute x4, starting transfers between devices, shifted_2(): return lax.ppermute(block, axis, route)  30.8 us
    ppermute x4, waiting for transfers between devices, shifted_2(): return lax.ppermute(block, axis, route)  15.1 us
    ppermute x4, starting transfers between devices, extended(): lax.ppermute(tail, axis, [(i, (i + 1) % count) for i in range(count)])  7.68 us
    ppermute x4, waiting for transfers between devices, extended(): lax.ppermute(head, axis, [((i + 1) % count, i) for i in range(count)])  3.25 us
  transfers between devices with their start and end apart: 12, of which 4 were waited for; matrix products, arithmetic and copies ran while one was open for 6% of the time, Pallas kernels for 0%

commit v1 on v0

v1 whole, which is shorter than its diff:
```python
import functools

import jax
import jax.numpy as jnp
from jax import lax
from jax.experimental import pallas as pl
from jax.experimental.pallas import tpu as pltpu
from jax.sharding import PartitionSpec as P

MESH = pl.DeviceIdType.MESH
F32 = jnp.float32

velocities = (
    (0, 0, 0),
    (1, 0, 0),
    (-1, 0, 0),
    (0, 1, 0),
    (0, -1, 0),
    (0, 0, 1),
    (0, 0, -1),
    (1, 1, 0),
    (-1, -1, 0),
    (1, -1, 0),
    (-1, 1, 0),
    (1, 0, 1),
    (-1, 0, -1),
    (1, 0, -1),
    (-1, 0, 1),
    (0, 1, 1),
    (0, -1, -1),
    (0, 1, -1),
    (0, -1, 1),
)
opposite = (0, 2, 1, 4, 3, 6, 5, 8, 7, 10, 9, 12, 11, 14, 13, 16, 15, 18, 17)
slot = {(0, 0): 0, (1, 1): 1, (2, 2): 2, (0, 1): 3, (1, 0): 3, (0, 2): 4, (2, 0): 4, (1, 2): 5, (2, 1): 5}
pairs = ((0, 0), (1, 1), (2, 2), (0, 1), (0, 2), (1, 2))
inlet_speed = 0.05
smooth_square = 0.02 * 0.02
F_CONF, F_COL, F_COT, F_UPW, F_G, F_K, F_W, F_R, F_CHI, F_ALL = 0, 6, 7, 12, 18, 21, 27, 30, 31, 32
C_OWN, C_Z, C_ZIN, C_X, C_XIN, C_CONF, C_COL, C_ALL = 0, 1, 4, 5, 8, 9, 15, 16


def dirs_where(axis, sign):
    return tuple(i for i in range(19) if velocities[i][axis] == sign)


def corner_dir(sx, sz):
    return next(i for i in range(19) if velocities[i][0] == sx and velocities[i][2] == sz)


def edge_dirs(axis, sign, other):
    return tuple(i for i in range(19) if velocities[i][axis] == sign and velocities[i][other] == 0)


def stress_of(conf):
    out = []
    for a, b in pairs:
        dot = conf[slot[a, 0]] * conf[slot[0, b]]
        for m in (1, 2):
            dot = dot + conf[slot[a, m]] * conf[slot[m, b]]
        out.append(conf[slot[a, b]] + 0.5 * dot)
    return out


def total(terms):
    result = None
    for sign, value in terms:
        if result is None:
            result = value if sign > 0 else -value
        else:
            result = result + value if sign > 0 else result - value
    return result


def moments(values):
    def weighted(sign_of):
        axial = total([(sign_of(velocities[i]), v) for i, v in values if 0 < i < 7 and sign_of(velocities[i])])
        edge = total([(sign_of(velocities[i]), v) for i, v in values if i >= 7 and sign_of(velocities[i])])
        if axial is None and edge is None:
            return None
        if axial is None:
            return edge * (1.0 / 36.0)
        if edge is None:
            return axial * (1.0 / 18.0)
        return axial * (1.0 / 18.0) + edge * (1.0 / 36.0)

    zeroth = weighted(lambda c: 1)
    rest = [v for i, v in values if i == 0]
    if rest:
        zeroth = zeroth + rest[0] * (1.0 / 3.0)
    first = [weighted(lambda c, a=a: c[a]) for a in range(3)]
    second = [weighted(lambda c, a=a, b=b: c[a] * c[b]) for a, b in pairs]
    return zeroth, first, second


def tensor_of(zeroth, second):
    out = []
    for k in range(6):
        value = None if second[k] is None else 9.0 * second[k]
        if k < 3:
            value = -3.0 * zeroth if value is None else value - 3.0 * zeroth
        out.append(value)
    return out


def apply(tensor, vector):
    out = []
    for a in range(3):
        value = None
        for b in range(3):
            if tensor[slot[a, b]] is not None:
                term = tensor[slot[a, b]] * vector[b]
                value = term if value is None else value + term
        out.append(value)
    return out


def plus(a, b):
    return a if b is None else b if a is None else a + b


def in_y(value, by):
    return value if by == 0 else pltpu.roll(value, (-by) % 128, 1)


def rows_of(row):
    return jnp.broadcast_to(row, (8, 128))


def kernel(
    pop, col, conf, lab, cot, con,
    o_pop, o_col, o_conf,
    v_pop, v_col, v_conf, v_lab, v_cot, v_con,
    snd, rcv, csnd, crcv,
    x_cot, x_conf, x_col, x_str, x_h, x_up, x_down, z_cot, z_str, z_h, v_u, v_ri,
    in_sem, f_send, f_recv, c_send, c_recv,
):
    loads = [
        pltpu.make_async_copy(src, dst, in_sem.at[k])
        for k, (src, dst) in enumerate(
            [(conf, v_conf), (col, v_col), (cot, v_cot), (pop, v_pop), (lab, v_lab), (con, v_con)]
        )
    ]
    for copy in loads:
        copy.start()
    nz, nx = lax.axis_size("gz"), lax.axis_size("xy")
    z, x = lax.axis_index("gz"), lax.axis_index("xy")
    z_of = {-1: lax.rem(z + nz - 1, nz), 0: z, 1: lax.rem(z + 1, nz)}
    x_of = {-1: lax.rem(x + nx - 1, nx), 0: x, 1: lax.rem(x + 1, nx)}
    faces = ((0, -1), (0, 1), (2, -1), (2, 1))
    face_device = [(z_of[0], x_of[-1]), (z_of[0], x_of[1]), (z_of[-1], x_of[0]), (z_of[1], x_of[0])]
    corners = ((-1, -1), (-1, 1), (1, -1), (1, 1))
    corner_device = [(z_of[cz], x_of[cx]) for cx, cz in corners]
    barrier = pltpu.get_barrier_semaphore()
    for device in face_device + corner_device:
        pl.semaphore_signal(barrier, inc=1, device_id=device, device_id_type=MESH)
    for copy in loads:
        copy.wait()

    lane = lax.broadcasted_iota(jnp.int32, (8, 128), 0)
    first, last = lane == 0, lane == 7

    def shift(value, by, low=None, high=None):
        if by == 0:
            return value
        rolled = pltpu.roll(value, 7 if by > 0 else 1, 0)
        fill = high if by > 0 else low
        fill = 0.0 if fill is None else fill
        return jnp.where(last if by > 0 else first, fill, rolled)

    def plane(ref, axis, at, k=None):
        rows = pl.ds(8 * at, 8) if axis == 0 else pl.ds(at, 8, stride=8)
        return ref[rows, :] if k is None else ref[k, rows, :]

    def flow_of(load):
        f = [load(i) for i in range(19)]
        rho = f[0]
        for i in range(1, 19):
            rho = rho + f[i]
        inverse = 1.0 / rho
        u = [total([(velocities[i][a], f[i]) for i in range(19) if velocities[i][a]]) * inverse for a in range(3)]
        return rho, inverse, u

    def make_face(index):
        axis, side = faces[index]
        across = 2 - axis
        edge = 7 if side > 0 else 0
        inner = edge - side
        p_edge = [plane(v_conf, axis, edge, k) for k in range(6)]
        p_inner = [plane(v_conf, axis, inner, k) for k in range(6)]
        s_edge, s_inner = stress_of(p_edge), stress_of(p_inner)
        c_edge, c_inner = plane(v_col, axis, edge), plane(v_col, axis, inner)
        _, inverse, u = flow_of(lambda i: plane(v_pop, axis, edge, i))
        ratio = 0.6875 * inverse
        fluid = jnp.where(plane(v_lab, axis, edge) == 0, 1.0, 0.0)
        out = snd.at[index]
        for k in range(6):
            out[F_CONF + k] = p_edge[k]
        out[F_COL] = c_edge
        for j, i in enumerate(dirs_where(axis, -side)):
            out[F_COT + j] = plane(v_cot, axis, edge, i)
        speed = u[axis] * u[axis] + smooth_square
        speed = speed * lax.rsqrt(speed)
        upwind = 0.25 * (speed - side * u[axis])
        for k in range(6):
            out[F_UPW + k] = upwind * plane(v_con, axis, edge, k)
        values = []
        for i in range(19):
            c = velocities[i]
            if c[axis] == side:
                continue
            got = plane(v_cot, axis, edge if c[axis] == 0 else inner, i)
            values.append((i, in_y(shift(got, c[across]), c[1])))
        zeroth, one, two = moments(values)
        tensor = tensor_of(zeroth, two)
        mobility = 1.0 - c_edge * c_edge
        force = []
        for a in range(3):
            k = slot[a, 1]
            value = 0.5 * (in_y(s_edge[k], 1) - in_y(s_edge[k], -1))
            k = slot[a, across]
            value = value + 0.5 * (shift(s_edge[k], 1) - shift(s_edge[k], -1))
            value = value - (0.5 * side) * s_inner[slot[a, axis]]
            if a == 1:
                slope = 0.5 * (in_y(c_edge, 1) - in_y(c_edge, -1))
            elif a == across:
                slope = 0.5 * (shift(c_edge, 1) - shift(c_edge, -1))
            else:
                slope = (-0.5 * side) * c_inner
            force.append(value + mobility * slope)
        for a in range(3):
            out[F_G + a] = one[a]
            out[F_W + a] = u[a] + ratio * force[a]
        for k in range(6):
            out[F_K + k] = tensor[k]
        out[F_R] = ratio
        out[F_CHI] = fluid

    def make_corner(index):
        cx, cz = corners[index]
        ex, ez = (7 if cx > 0 else 0), (7 if cz > 0 else 0)
        here = pl.ds(8 * ex + ez, 1)
        in_x, in_z = pl.ds(8 * (ex - cx) + ez, 1), pl.ds(8 * ex + ez - cz, 1)
        diagonal = corner_dir(-cx, -cz)

        def put(row, value):
            csnd[index, pl.ds(row, 1), :] = value

        put(C_OWN, v_cot[diagonal, here, :])
        for j, i in enumerate(edge_dirs(2, -cz, 0)):
            put(C_Z + j, v_cot[i, here, :])
        put(C_ZIN, v_cot[diagonal, in_x, :])
        for j, i in enumerate(edge_dirs(0, -cx, 2)):
            put(C_X + j, v_cot[i, here, :])
        put(C_XIN, v_cot[diagonal, in_z, :])
        for k in range(6):
            put(C_CONF + k, v_conf[k, here, :])
        put(C_COL, v_col[here, :])

    for index in range(4):
        make_face(index)
    for index in range(4):
        make_corner(index)
    pl.semaphore_wait(barrier, 8)
    face_copies = [
        pltpu.make_async_remote_copy(
            src_ref=snd.at[k], dst_ref=rcv.at[k ^ 1], send_sem=f_send.at[k], recv_sem=f_recv.at[k ^ 1],
            device_id=face_device[k], device_id_type=MESH,
        )
        for k in range(4)
    ]
    corner_copies = [
        pltpu.make_async_remote_copy(
            src_ref=csnd.at[k], dst_ref=crcv.at[3 - k], send_sem=c_send.at[k], recv_sem=c_recv.at[3 - k],
            device_id=corner_device[k], device_id_type=MESH,
        )
        for k in range(4)
    ]
    for copy in face_copies + corner_copies:
        copy.start()

    def local(at, carry):
        rows, padded = pl.ds(pl.multiple_of(8 * at, 8), 8), pl.ds(pl.multiple_of(8 * at + 8, 8), 8)
        p = [v_conf[k, rows, :] for k in range(6)]
        s = stress_of(p)
        for k in range(6):
            x_conf[k, padded, :] = p[k]
            x_str[k, padded, :] = s[k]
        x_col[padded, :] = v_col[rows, :]
        for i in range(19):
            x_cot[i, padded, :] = v_cot[i, rows, :]
        _, inverse, u = flow_of(lambda i: v_pop[i, rows, :])
        for a in range(3):
            v_u[a, rows, :] = u[a]
        v_ri[rows, :] = inverse
        square = u[0] * u[0] + smooth_square
        speed = square * lax.rsqrt(square)
        up, down = 0.25 * (speed - u[0]), 0.25 * (speed + u[0])
        for k in range(6):
            q = v_con[k, rows, :]
            x_up[k, padded, :] = up * q
            x_down[k, padded, :] = down * q
        return carry

    lax.fori_loop(0, 8, local, 0)

    for copy in face_copies + corner_copies:
        copy.wait_recv()

    for side, index in ((-1, 0), (1, 1)):
        rows = pl.ds(0 if side < 0 else 72, 8)
        got = rcv.at[index]
        p = [got[F_CONF + k] for k in range(6)]
        s = stress_of(p)
        for k in range(6):
            x_conf[k, rows, :] = p[k]
            x_str[k, rows, :] = s[k]
        x_col[rows, :] = got[F_COL]
        for j, i in enumerate(dirs_where(0, side)):
            x_cot[i, rows, :] = got[F_COT + j]
        for k in range(6):
            (x_up if side < 0 else x_down)[k, rows, :] = got[F_UPW + k]
    for n, (side, index) in enumerate(((-1, 2), (1, 3))):
        got = rcv.at[index]
        for j, i in enumerate(dirs_where(2, side)):
            z_cot[n, j, pl.ds(8, 8), :] = got[F_COT + j]
            for cx in (-1, 1):
                if velocities[i][0] == cx:
                    z_cot[n, j, pl.ds(7 if cx < 0 else 16, 1), :] = crcv[corners.index((cx, side)), pl.ds(C_OWN, 1), :]
        s = stress_of([got[F_CONF + k] for k in range(6)])
        for a in range(3):
            z_str[n, a] = s[slot[a, 2]]

    def halo_force(index):
        axis, side = faces[index]
        across = 2 - axis
        edge = 0 if side < 0 else 7
        got = rcv.at[index]

        def corner_at(end):
            place = (side, end) if axis == 0 else (end, side)
            return corners.index(place)

        ends = {-1: first, 1: last}
        fills = {}
        for end in (-1, 1):
            c = corner_at(end)
            p = [crcv[c, pl.ds(C_CONF + k, 1), :] for k in range(6)]
            s = stress_of(p)
            fills[end] = ([s[slot[a, across]] for a in range(3)], crcv[c, pl.ds(C_COL, 1), :])
        c_halo = got[F_COL]
        mobility = 1.0 - c_halo * c_halo
        low, high = fills[-1], fills[1]

        def at_ends(lo, hi):
            return jnp.where(first, rows_of(-0.5 * lo), jnp.where(last, rows_of(0.5 * hi), 0.0))

        p = [plane(v_conf, axis, edge, k) for k in range(6)]
        s = stress_of(p)
        c_edge = plane(v_col, axis, edge)
        force = []
        for a in range(3):
            value = (-0.5 * side) * s[slot[a, axis]] + at_ends(low[0][a], high[0][a])
            if a == axis:
                value = value + mobility * ((-0.5 * side) * c_edge)
            elif a == across:
                value = value + mobility * at_ends(low[1], high[1])
            force.append(value)
        values = []
        for i in dirs_where(axis, -side):
            c = velocities[i]
            value = plane(v_cot, axis, edge, i)
            if c[across]:
                end = c[across]
                if axis == 0:
                    n = 0 if end < 0 else 1
                    j = dirs_where(2, end).index(i)
                    row = z_cot[n, j, pl.ds(8 + edge, 1), :]
                else:
                    row = x_cot[i, pl.ds((0 if end < 0 else 72) + edge, 1), :]
                value = shift(value, end, rows_of(row), rows_of(row))
            values.append((i, in_y(value, c[1])))
        for end in (-1, 1):
            c = corner_at(end)
            base = C_Z if axis == 0 else C_X
            for j, i in enumerate(edge_dirs(across, end, axis)):
                row = crcv[c, pl.ds(base + j, 1), :]
                values.append((i, in_y(jnp.where(ends[end], rows_of(row), 0.0), velocities[i][1])))
            i = corner_dir(side, end) if axis == 0 else corner_dir(end, side)
            row = crcv[c, pl.ds(C_ZIN if axis == 0 else C_XIN, 1), :]
            values.append((i, jnp.where(ends[end], rows_of(row), 0.0)))
        zeroth, one, two = moments(values)
        tensor = tensor_of(zeroth, two)
        one = [plus(one[a], got[F_G + a]) for a in range(3)]
        tensor = [plus(tensor[k], got[F_K + k]) for k in range(6)]
        ratio = got[F_R]
        w = [got[F_W + a] + ratio * force[a] for a in range(3)]
        turned = apply(tensor, w)
        return [got[F_CHI] * (3.0 * one[a] + turned[a]) for a in range(3)]

    for index in range(4):
        h = halo_force(index)
        for a in range(3):
            if index < 2:
                x_h[a, pl.ds(0 if index == 0 else 72, 8), :] = h[a]
            else:
                z_h[index - 2, a] = h[a]

    def main(at, carry):
        def rows(by=0):
            return pl.ds(pl.multiple_of(8 * (at + by), 8), 8)

        def padded(by=0):
            return pl.ds(pl.multiple_of(8 * (at + by) + 8, 8), 8)

        def z_row(ref, n, k):
            return rows_of(ref[n, k, pl.ds(at, 1), :])

        def face_row(index, k):
            return rows_of(rcv[index, k, pl.ds(at, 1), :])

        label = v_lab[rows(), :]
        fluid = jnp.where(label == 0, 1.0, 0.0)
        solid = label == 1
        inverse = v_ri[rows(), :]
        u = [v_u[a, rows(), :] for a in range(3)]
        colour = x_col[padded(), :]
        mobility = 1.0 - colour * colour
        force = []
        for a in range(3):
            k = slot[a, 0]
            value = x_str[k, padded(1), :] - x_str[k, padded(-1), :]
            k = slot[a, 1]
            here = x_str[k, padded(), :]
            value = value + (in_y(here, 1) - in_y(here, -1))
            here = x_str[slot[a, 2], padded(), :]
            value = value + (shift(here, 1, None, z_row(z_str, 1, a)) - shift(here, -1, z_row(z_str, 0, a), None))
            if a == 0:
                slope = x_col[padded(1), :] - x_col[padded(-1), :]
            elif a == 1:
                slope = in_y(colour, 1) - in_y(colour, -1)
            else:
                slope = shift(colour, 1, None, face_row(3, F_COL)) - shift(colour, -1, face_row(2, F_COL), None)
            force.append(0.5 * (value + mobility * slope))
        values = []
        for i in range(19):
            c = velocities[i]
            value = x_cot[i, padded(c[0]), :]
            if c[2]:
                n = 0 if c[2] < 0 else 1
                row = rows_of(z_cot[n, dirs_where(2, c[2]).index(i), pl.ds(8 + at + c[0], 1), :])
                value = shift(value, c[2], row, row)
            values.append((i, in_y(value, c[1])))
        zeroth, one, two = moments(values)
        tensor = tensor_of(zeroth, two)
        v = [u[a] + 0.5 * inverse * force[a] for a in range(3)]
        turned = apply(tensor, v)
        lean = [3.0 * one[a] + turned[a] for a in range(3)]
        energy = zeroth
        for a in range(3):
            energy = energy + v[a] * (3.0 * one[a] + 0.5 * turned[a])
        other = apply(tensor, force)
        h = [fluid * (lean[a] + (0.1875 * inverse) * other[a]) for a in range(3)]
        pull = [fluid * (1.25 * lean[a] + (0.375 * inverse) * other[a]) for a in range(3)]
        for a in range(3):
            x_h[a, padded(), :] = h[a]
        rho_bar = (1.25 * fluid) * energy
        for a in range(3):
            rho_bar = rho_bar - (0.5 * inverse) * (pull[a] * force[a])
        inlet = (
            (1.0 - 1.5 * inlet_speed * inlet_speed) * zeroth
            + (3.0 * inlet_speed) * one[2]
            + (4.5 * inlet_speed * inlet_speed) * two[2]
        )
        rho_bar = rho_bar + jnp.where(label == 2, inlet, 0.0)
        q = [v_con[k, rows(), :] for k in range(6)]
        m_bar = []
        for a in range(3):
            along = bend = None
            for k in range(6):
                here = x_conf[k, padded(), :]
                if a == 0:
                    up, down = x_conf[k, padded(1), :], x_conf[k, padded(-1), :]
                elif a == 1:
                    up, down = in_y(here, 1), in_y(here, -1)
                else:
                    up = shift(here, 1, None, face_row(3, F_CONF + k))
                    down = shift(here, -1, face_row(2, F_CONF + k), None)
                d, c = q[k] * (up - down), q[k] * (up + down - 2.0 * here)
                along, bend = plus(along, d), plus(bend, c)
            square = u[a] * u[a] + smooth_square
            u_bar = (0.25 * u[a] * lax.rsqrt(square)) * bend - 0.25 * along
            m_bar.append(pull[a] + inverse * u_bar)
        for a in range(3):
            rho_bar = rho_bar - m_bar[a] * u[a]
        keep = -0.25 * fluid
        by_dir = dict(values)
        for i in range(19):
            c = velocities[i]
            value = rho_bar + jnp.where(solid, by_dir[opposite[i]], keep * by_dir[i])
            for a in range(3):
                if c[a]:
                    value = value + m_bar[a] if c[a] > 0 else value - m_bar[a]
            o_pop[i, rows(), :] = value
        return carry

    lax.fori_loop(0, 8, main, 0)

    def finish(at, carry):
        def rows(by=0):
            return pl.ds(pl.multiple_of(8 * (at + by), 8), 8)

        def padded(by=0):
            return pl.ds(pl.multiple_of(8 * (at + by) + 8, 8), 8)

        h = [x_h[a, padded(), :] for a in range(3)]
        u = [v_u[a, rows(), :] for a in range(3)]
        colour = x_col[padded(), :]
        mobility = 1.0 - colour * colour
        t = []
        colour_bar = None
        for a in range(3):
            row_down = rows_of(z_h[0, a, pl.ds(at, 1), :])
            row_up = rows_of(z_h[1, a, pl.ds(at, 1), :])
            t.append(
                [
                    x_h[a, padded(-1), :] - x_h[a, padded(1), :],
                    in_y(h[a], -1) - in_y(h[a], 1),
                    shift(h[a], -1, row_down, None) - shift(h[a], 1, None, row_up),
                ]
            )
        def flux(by):
            near = x_col[padded(by), :]
            return (1.0 - near * near) * x_h[0, padded(by), :]

        up_c, down_c = x_col[padded(1), :], x_col[padded(-1), :]
        z_up_c, z_down_c = rows_of(rcv[3, F_COL, pl.ds(at, 1), :]), rows_of(rcv[2, F_COL, pl.ds(at, 1), :])
        slopes = [
            up_c - down_c,
            in_y(colour, 1) - in_y(colour, -1),
            shift(colour, 1, None, z_up_c) - shift(colour, -1, z_down_c, None),
        ]
        colour_bar = h[0] * slopes[0] + h[1] * slopes[1] + h[2] * slopes[2]
        colour_bar = -colour * colour_bar
        in_z = mobility * h[2]
        z_up_f = (1.0 - z_up_c * z_up_c) * rows_of(z_h[1, 2, pl.ds(at, 1), :])
        z_down_f = (1.0 - z_down_c * z_down_c) * rows_of(z_h[0, 2, pl.ds(at, 1), :])
        flow_y = mobility * h[1]
        spread = (
            (flux(-1) - flux(1))
            + (in_y(flow_y, -1) - in_y(flow_y, 1))
            + (shift(in_z, -1, z_down_f, None) - shift(in_z, 1, None, z_up_f))
        )
        o_col[rows(), :] = colour_bar + 0.5 * spread
        w = []
        for a, b in pairs:
            w.append(0.5 * t[a][a] if a == b else 0.25 * (t[a][b] + t[b][a]))
        p = [x_conf[k, padded(), :] for k in range(6)]
        result = []
        for a, b in pairs:
            dot = None
            for m in range(3):
                if a == b:
                    dot = plus(dot, w[slot[a, m]] * p[slot[m, b]])
                else:
                    dot = plus(dot, w[slot[a, m]] * p[slot[m, b]] + p[slot[a, m]] * w[slot[m, b]])
            result.append(w[slot[a, b]] + dot if a == b else 2.0 * w[slot[a, b]] + dot)
        speeds = []
        for a in range(3):
            square = u[a] * u[a] + smooth_square
            speeds.append(square * lax.rsqrt(square))
        stay = 0.9 - 0.5 * (speeds[0] + speeds[1] + speeds[2])
        go_up = [0.25 * (speeds[a] - u[a]) for a in range(3)]
        go_down = [0.25 * (speeds[a] + u[a]) for a in range(3)]
        for k in range(6):
            q = v_con[k, rows(), :]
            value = result[k] + stay * q
            value = value + in_y(go_up[1] * q, -1) + in_y(go_down[1] * q, 1)
            value = value + shift(go_up[2] * q, -1, rows_of(rcv[2, F_UPW + k, pl.ds(at, 1), :]), None)
            value = value + shift(go_down[2] * q, 1, None, rows_of(rcv[3, F_UPW + k, pl.ds(at, 1), :]))
            value = value + x_up[k, padded(-1), :] + x_down[k, padded(1), :]
            o_conf[k, rows(), :] = value
        return carry

    lax.fori_loop(0, 8, finish, 0)
    for copy in face_copies + corner_copies:
        copy.wait_send()


def deliver(a, b, c, out_a, out_b, out_c, sem):
    copies = [
        pltpu.make_async_copy(src, dst, sem.at[k]) for k, (src, dst) in enumerate(((a, out_a), (b, out_b), (c, out_c)))
    ]
    for copy in copies:
        copy.start()
    for copy in copies:
        copy.wait()


def body(populations, colour, conformation, labels, pop_cotangent, conf_cotangent):
    anywhere = pl.BlockSpec(memory_space=pl.ANY)
    near = pl.BlockSpec(memory_space=pltpu.VMEM)
    args = [
        v.reshape(v.shape[:-3] + (64, 128))
        for v in (populations, colour, conformation, labels, pop_cotangent, conf_cotangent)
    ]
    shapes = [(19, 64, 128), (64, 128), (6, 64, 128)]
    scratch = [pltpu.VMEM(v.shape, v.dtype) for v in args]
    scratch += [pltpu.VMEM((4, F_ALL, 8, 128), F32)] * 2
    scratch += [pltpu.VMEM((4, C_ALL, 128), F32)] * 2
    padded = [(19, 80, 128), (6, 80, 128), (80, 128), (6, 80, 128), (3, 80, 128), (6, 80, 128), (6, 80, 128)]
    scratch += [pltpu.VMEM(s, F32) for s in padded]
    scratch += [pltpu.VMEM(s, F32) for s in [(2, 5, 24, 128), (2, 3, 8, 128), (2, 3, 8, 128), (3, 64, 128), (64, 128)]]
    scratch += [pltpu.SemaphoreType.DMA((6,))] + [pltpu.SemaphoreType.DMA((4,))] * 4
    parts = pl.pallas_call(
        kernel,
        out_shape=tuple(pltpu.VMEM(s, F32) for s in shapes),
        in_specs=[anywhere] * 6,
        out_specs=[near] * 3,
        scratch_shapes=scratch,
        compiler_params=pltpu.CompilerParams(
            collective_id=0, has_side_effects=True, vmem_limit_bytes=32 * 1024 * 1024
        ),
    )(*[pltpu.with_memory_space_constraint(v, pltpu.HBM) for v in args])
    parts = [pltpu.with_memory_space_constraint(v, pltpu.VMEM) for v in parts]
    out = pl.pallas_call(
        deliver,
        out_shape=tuple(jax.ShapeDtypeStruct(s, F32) for s in shapes),
        in_specs=[near] * 3,
        out_specs=[anywhere] * 3,
        scratch_shapes=[pltpu.SemaphoreType.DMA((3,))],
    )(*parts)
    return tuple(v.reshape(v.shape[:-2] + (8, 8, 128)) for v in out)


def solution(mesh):
    placed = (
        P(None, "xy", "gz", None),
        P("xy", "gz", None),
        P(None, "xy", "gz", None),
        P("xy", "gz", None),
        P(None, "xy", "gz", None),
        P(None, "xy", "gz", None),
    )
    return jax.shard_map(
        body,
        mesh=mesh,
        in_specs=placed,
        out_specs=(P(None, "xy", "gz", None), P("xy", "gz", None), P(None, "xy", "gz", None)),
        check_vma=False,
    )
```

time: 126 us -> 35.2 us (0.28)
  starting transfers between devices: 87 us -> 0 us
  Pallas kernels: 0 us -> 34.4 us
  waiting for transfers between devices: 18.6 us -> 0 us
  other arithmetic: 10.1 us -> 0 us
  local copies, waits for them, and re-layouts: 8.14 us -> 0 us
    ppermute x12 -> x0, starting transfers between devices: 87 us -> none  [the longest x4 48.5 us: extended(): lax.ppermute(head, axis, [((i + 1) % count, i) for i in range(count)])]
    pallas_call x0 -> x2, Pallas kernels: none -> 34.4 us  [the longest x1 33.5 us: body(): pl.pallas_call(kernel, out_shape=tuple((pltpu.VMEM(s, F32) for s in shape...]
    ppermute x12 -> x0, waiting for transfers between devices: 18.6 us -> none  [the longest x4 15.1 us: shifted_2(): return lax.ppermute(block, axis, route)]
    add_any x15 -> x0, other arithmetic: 4.78 us -> none  [the longest x1 1.65 us: local_step(): velocity.append(moment / density)]
    slice x27 -> x0, local copies, waits for them, and re-layouts: 3.73 us -> none  [the longest x1 1.5 us: extended(): head = lax.slice_in_dim(cells, 0, width, axis=dim)]
    unnamed x28 -> x0, local copies, waits for them, and re-layouts: 1.62 us -> none
    neg x4 -> x0, other arithmetic: 1.48 us -> none  [the longest x1 0.68 us: axis_derivative(): return 0.5 * (padded[:, 1:-1, 2:, :] - padded[:, 1:-1, :-2, :])]
  transfers between devices with their start and end apart: 12 -> 0, of which waited for: 4 -> 0; matrix products, arithmetic and copies ran while one was open for 6% -> 0% of each run, Pallas kernels for 0% -> 0%
where the time goes in v1:
time: 35.2 us; the launch traced here: 35.1 us
  Pallas kernels  34.4 us (98%)
  between operations  0.64 us (2%)
    pallas_call x1, Pallas kernels, body(): pl.pallas_call(kernel, out_shape=tuple((pltpu.VMEM(s, F32) for s in shape...  33.5 us
    pallas_call x1, Pallas kernels, body(): pl.pallas_call(deliver, out_shape=tuple((jax.ShapeDtypeStruct(s, F32) for...  0.92 us

profile of v1, /device:TPU:32, one launch (start us, length us, event | category | flops | bytes accessed | tf_op | source)
XLA Modules:
  0.0 35.1 jit_solution(2760480358826523119)
XLA Ops:
  0.6 33.5 %shard_map.85 = (f32[19,64,128]{2,1,0:T(8,128)S(1)}, f32[64,128]{1,0:T(8,128)S(1)}, f32[6,64,128]{2,1,0:T(8,128)S(1)}) custom-call(f32[19,64,128]{2,1,0:T(8,128)} %bitcast.9, f32[64,128]{1,0:T(8,128)} %bitcast.13, f32[6,64,128]{2,1,0:T(8,128)} %bitcast.11, s32[64,128]{1,0:T(8,128)} %bitcast.14, f32[19,64,128]{2,1,0:T(8,128)} %bitcast.10, f32[6,64,128]{2,1,0:T(8,128)} %bitcast.12), custom_call_target="tpu_custom_call" | custom-call | tf_op jit(solution)/shard_map/pallas_call | solution.py:615
  34.1 0.9 %shard_map.86 = (f32[19,64,128]{2,1,0:T(8,128)}, f32[64,128]{1,0:T(8,128)}, f32[6,64,128]{2,1,0:T(8,128)}) custom-call(f32[19,64,128]{2,1,0:T(8,128)S(1)} %get-tuple-element.9.a, f32[64,128]{1,0:T(8,128)S(1)} %get-tuple-element.10.b, f32[6,64,128]{2,1,0:T(8,128)S(1)} %get-tuple-element.11.c), custom_call_target="tpu_custom_call" | custom-call | tf_op jit(solution)/shard_map/pallas_call | solution.py:626

commit v2 on v1

--- a/solution.py
+++ b/solution.py
@@ -133,7 +133,7 @@
     v_pop, v_col, v_conf, v_lab, v_cot, v_con,
     snd, rcv, csnd, crcv,
     x_cot, x_conf, x_col, x_str, x_h, x_up, x_down, z_cot, z_str, z_h, v_u, v_ri,
-    in_sem, f_send, f_recv, c_send, c_recv,
+    in_sem, f_send, f_recv, c_send, c_recv, go_sem,
 ):
     loads = [
         pltpu.make_async_copy(src, dst, in_sem.at[k])
@@ -151,9 +151,32 @@
     face_device = [(z_of[0], x_of[-1]), (z_of[0], x_of[1]), (z_of[-1], x_of[0]), (z_of[1], x_of[0])]
     corners = ((-1, -1), (-1, 1), (1, -1), (1, 1))
     corner_device = [(z_of[cz], x_of[cx]) for cx, cz in corners]
+    place = lax.rem(x, 8)
+    upper = lax.rem(lax.div(x, 8), 2)
+    edge_x = {-1: place == 0, 0: False, 1: place == 7}
+    edge_z = {-1: z == 0, 0: False, 1: z == nz - 1}
+    offsets = [((side, 0) if axis == 0 else (0, side)) for axis, side in faces] + list(corners)
+    devices = face_device + corner_device
+    flip = (1, 0, 3, 2, 7, 6, 5, 4)
+    follows, leads = [], []
+    for dx, dz in offsets:
+        far_x, far_z = edge_x[dx], edge_z[dz]
+        far = jnp.logical_or(far_x, far_z)
+        follow = jnp.logical_or(
+            jnp.logical_and(far_x, upper == 0),
+            jnp.logical_and(jnp.logical_and(far_z, jnp.logical_not(far_x)), z == 0),
+        )
+        follows.append(follow)
+        leads.append(jnp.logical_and(far, jnp.logical_not(follow)))
     barrier = pltpu.get_barrier_semaphore()
-    for device in face_device + corner_device:
-        pl.semaphore_signal(barrier, inc=1, device_id=device, device_id_type=MESH)
+    expected = jnp.int32(0)
+    for device, follow, lead in zip(devices, follows, leads):
+        expected = expected + jnp.where(follow, 0, 1)
+
+        @pl.when(jnp.logical_not(lead))
+        def _(device=device):
+            pl.semaphore_signal(barrier, inc=1, device_id=device, device_id_type=MESH)
+
     for copy in loads:
         copy.wait()
 
@@ -261,7 +284,7 @@
         make_face(index)
     for index in range(4):
         make_corner(index)
-    pl.semaphore_wait(barrier, 8)
+    pl.semaphore_wait(barrier, expected)
     face_copies = [
         pltpu.make_async_remote_copy(
             src_ref=snd.at[k], dst_ref=rcv.at[k ^ 1], send_sem=f_send.at[k], recv_sem=f_recv.at[k ^ 1],
@@ -276,8 +299,26 @@
         )
         for k in range(4)
     ]
-    for copy in face_copies + corner_copies:
-        copy.start()
+    copies = face_copies + corner_copies
+    for k in range(8):
+
+        @pl.when(leads[k])
+        def _(k=k):
+            pl.semaphore_signal(go_sem.at[flip[k]], inc=1, device_id=devices[k], device_id_type=MESH)
+
+    for copy, follow in zip(copies, follows):
+
+        @pl.when(jnp.logical_not(follow))
+        def _(copy=copy):
+            copy.start()
+
+    def send_later(ks):
+        for k in ks:
+
+            @pl.when(follows[k])
+            def _(k=k):
+                pl.semaphore_wait(go_sem.at[k], 1)
+                copies[k].start()
 
     def local(at, carry):
         rows, padded = pl.ds(pl.multiple_of(8 * at, 8), 8), pl.ds(pl.multiple_of(8 * at + 8, 8), 8)
@@ -304,8 +345,10 @@
 
     lax.fori_loop(0, 8, local, 0)
 
-    for copy in face_copies + corner_copies:
-        copy.wait_recv()
+    arrival = [copies[k] for k in flip]
+    send_later((2, 3, 4, 5, 6, 7, 0, 1))
+    for k in range(8):
+        arrival[k].wait_recv()
 
     for side, index in ((-1, 0), (1, 1)):
         rows = pl.ds(0 if side < 0 else 72, 8)
@@ -583,7 +626,7 @@
         return carry
 
     lax.fori_loop(0, 8, finish, 0)
-    for copy in face_copies + corner_copies:
+    for copy in copies:
         copy.wait_send()
 
 
@@ -612,6 +655,7 @@
     scratch += [pltpu.VMEM(s, F32) for s in padded]
     scratch += [pltpu.VMEM(s, F32) for s in [(2, 5, 24, 128), (2, 3, 8, 128), (2, 3, 8, 128), (3, 64, 128), (64, 128)]]
     scratch += [pltpu.SemaphoreType.DMA((6,))] + [pltpu.SemaphoreType.DMA((4,))] * 4
+    scratch += [pltpu.SemaphoreType.REGULAR((8,))]
     parts = pl.pallas_call(
         kernel,
         out_shape=tuple(pltpu.VMEM(s, F32) for s in shapes),

time: 35.2 us -> 32.6 us (0.926)
  the two profiles are of different devices: /device:TPU:32 before, /device:TPU:64 now
where the time goes in v2:
time: 32.6 us; the launch traced here: 32.5 us
  Pallas kernels  31.9 us (98%)
  between operations  0.64 us (2%)
    pallas_call x1, Pallas kernels, body(): pl.pallas_call(kernel, out_shape=tuple((pltpu.VMEM(s, F32) for s in shape...  30.9 us
    pallas_call x1, Pallas kernels, body(): pl.pallas_call(deliver, out_shape=tuple((jax.ShapeDtypeStruct(s, F32) for...  0.92 us

profile of v2, /device:TPU:64, one launch (start us, length us, event | category | flops | bytes accessed | tf_op | source)
XLA Modules:
  0.0 32.5 jit_solution(15115039195612178184)
XLA Ops:
  0.6 30.9 %shard_map.85 = (f32[19,64,128]{2,1,0:T(8,128)S(1)}, f32[64,128]{1,0:T(8,128)S(1)}, f32[6,64,128]{2,1,0:T(8,128)S(1)}) custom-call(f32[19,64,128]{2,1,0:T(8,128)} %bitcast.9, f32[64,128]{1,0:T(8,128)} %bitcast.13, f32[6,64,128]{2,1,0:T(8,128)} %bitcast.11, s32[64,128]{1,0:T(8,128)} %bitcast.14, f32[19,64,128]{2,1,0:T(8,128)} %bitcast.10, f32[6,64,128]{2,1,0:T(8,128)} %bitcast.12), custom_call_target="tpu_custom_call" | custom-call | tf_op jit(solution)/shard_map/pallas_call | solution.py:659
  31.6 0.9 %shard_map.86 = (f32[19,64,128]{2,1,0:T(8,128)}, f32[64,128]{1,0:T(8,128)}, f32[6,64,128]{2,1,0:T(8,128)}) custom-call(f32[19,64,128]{2,1,0:T(8,128)S(1)} %get-tuple-element.9.a, f32[64,128]{1,0:T(8,128)S(1)} %get-tuple-element.10.b, f32[6,64,128]{2,1,0:T(8,128)S(1)} %get-tuple-element.11.c), custom_call_target="tpu_custom_call" | custom-call | tf_op jit(solution)/shard_map/pallas_call | solution.py:670

commit v3 on v2

--- a/solution.py
+++ b/solution.py
@@ -9,6 +9,7 @@
 
 MESH = pl.DeviceIdType.MESH
 F32 = jnp.float32
+LEVEL = (3, 6)
 
 velocities = (
     (0, 0, 0),
@@ -123,6 +124,10 @@
     return value if by == 0 else pltpu.roll(value, (-by) % 128, 1)
 
 
+def eights(n):
+    return 8 * n if isinstance(n, int) else pl.multiple_of(8 * n, 8)
+
+
 def rows_of(row):
     return jnp.broadcast_to(row, (8, 128))
 
@@ -135,13 +140,22 @@
     x_cot, x_conf, x_col, x_str, x_h, x_up, x_down, z_cot, z_str, z_h, v_u, v_ri,
     in_sem, f_send, f_recv, c_send, c_recv, go_sem,
 ):
-    loads = [
-        pltpu.make_async_copy(src, dst, in_sem.at[k])
-        for k, (src, dst) in enumerate(
-            [(conf, v_conf), (col, v_col), (cot, v_cot), (pop, v_pop), (lab, v_lab), (con, v_con)]
-        )
-    ]
-    for copy in loads:
+    fields = [(conf, v_conf), (col, v_col), (cot, v_cot), (pop, v_pop), (lab, v_lab), (con, v_con)]
+
+    def load(group, begin, count):
+        rows = pl.ds(begin, count)
+        return [
+            pltpu.make_async_copy(
+                src.at[rows] if len(src.shape) == 2 else src.at[:, rows],
+                dst.at[rows] if len(dst.shape) == 2 else dst.at[:, rows],
+                in_sem.at[group, k],
+            )
+            for k, (src, dst) in enumerate(fields)
+        ]
+
+    outer = load(0, 0, 16) + load(1, 48, 16)
+    middle = load(2, 16, 32)
+    for copy in outer + middle:
         copy.start()
     nz, nx = lax.axis_size("gz"), lax.axis_size("xy")
     z, x = lax.axis_index("gz"), lax.axis_index("xy")
@@ -158,15 +172,18 @@
     offsets = [((side, 0) if axis == 0 else (0, side)) for axis, side in faces] + list(corners)
     devices = face_device + corner_device
     flip = (1, 0, 3, 2, 7, 6, 5, 4)
-    follows, leads = [], []
+    follows, leads, across_x = [], [], []
     for dx, dz in offsets:
         far_x, far_z = edge_x[dx], edge_z[dz]
-        far = jnp.logical_or(far_x, far_z)
+        level = jnp.logical_and(jnp.minimum(z, z + dz) >= LEVEL[0], jnp.maximum(z, z + dz) <= LEVEL[1])
+        far_x_led = jnp.logical_and(far_x, jnp.logical_not(level))
+        far = jnp.logical_or(far_x_led, far_z)
         follow = jnp.logical_or(
-            jnp.logical_and(far_x, upper == 0),
+            jnp.logical_and(far_x_led, upper == 0),
             jnp.logical_and(jnp.logical_and(far_z, jnp.logical_not(far_x)), z == 0),
         )
         follows.append(follow)
+        across_x.append(far_x)
         leads.append(jnp.logical_and(far, jnp.logical_not(follow)))
     barrier = pltpu.get_barrier_semaphore()
     expected = jnp.int32(0)
@@ -177,8 +194,6 @@
         def _(device=device):
             pl.semaphore_signal(barrier, inc=1, device_id=device, device_id_type=MESH)
 
-    for copy in loads:
-        copy.wait()
 
     lane = lax.broadcasted_iota(jnp.int32, (8, 128), 0)
     first, last = lane == 0, lane == 7
@@ -280,11 +295,6 @@
             put(C_CONF + k, v_conf[k, here, :])
         put(C_COL, v_col[here, :])
 
-    for index in range(4):
-        make_face(index)
-    for index in range(4):
-        make_corner(index)
-    pl.semaphore_wait(barrier, expected)
     face_copies = [
         pltpu.make_async_remote_copy(
             src_ref=snd.at[k], dst_ref=rcv.at[k ^ 1], send_sem=f_send.at[k], recv_sem=f_recv.at[k ^ 1],
@@ -300,25 +310,42 @@
         for k in range(4)
     ]
     copies = face_copies + corner_copies
+    arrival = [copies[k] for k in flip]
+
+    def send(ks):
+        for k in ks:
+
+            @pl.when(jnp.logical_not(follows[k]))
+            def _(k=k):
+                copies[k].start()
+
+    def send_later(ks, over_x):
+        for k in ks:
+
+            @pl.when(jnp.logical_and(follows[k], jnp.equal(across_x[k], over_x)))
+            def _(k=k):
+                pl.semaphore_wait(go_sem.at[k], 1)
+                copies[k].start()
+
+    for copy in outer:
+        copy.wait()
+    make_face(0)
+    make_face(1)
+    pl.semaphore_wait(barrier, expected)
     for k in range(8):
 
         @pl.when(leads[k])
         def _(k=k):
             pl.semaphore_signal(go_sem.at[flip[k]], inc=1, device_id=devices[k], device_id_type=MESH)
 
-    for copy, follow in zip(copies, follows):
-
-        @pl.when(jnp.logical_not(follow))
-        def _(copy=copy):
-            copy.start()
-
-    def send_later(ks):
-        for k in ks:
-
-            @pl.when(follows[k])
-            def _(k=k):
-                pl.semaphore_wait(go_sem.at[k], 1)
-                copies[k].start()
+    send((0, 1))
+    for copy in middle:
+        copy.wait()
+    for index in range(4):
+        make_corner(index)
+    make_face(2)
+    make_face(3)
+    send((4, 5, 6, 7, 3, 2))
 
     def local(at, carry):
         rows, padded = pl.ds(pl.multiple_of(8 * at, 8), 8), pl.ds(pl.multiple_of(8 * at + 8, 8), 8)
@@ -345,36 +372,36 @@
 
     lax.fori_loop(0, 8, local, 0)
 
-    arrival = [copies[k] for k in flip]
-    send_later((2, 3, 4, 5, 6, 7, 0, 1))
-    for k in range(8):
-        arrival[k].wait_recv()
-
-    for side, index in ((-1, 0), (1, 1)):
-        rows = pl.ds(0 if side < 0 else 72, 8)
-        got = rcv.at[index]
-        p = [got[F_CONF + k] for k in range(6)]
-        s = stress_of(p)
-        for k in range(6):
-            x_conf[k, rows, :] = p[k]
-            x_str[k, rows, :] = s[k]
-        x_col[rows, :] = got[F_COL]
-        for j, i in enumerate(dirs_where(0, side)):
-            x_cot[i, rows, :] = got[F_COT + j]
-        for k in range(6):
-            (x_up if side < 0 else x_down)[k, rows, :] = got[F_UPW + k]
-    for n, (side, index) in enumerate(((-1, 2), (1, 3))):
-        got = rcv.at[index]
-        for j, i in enumerate(dirs_where(2, side)):
-            z_cot[n, j, pl.ds(8, 8), :] = got[F_COT + j]
+    def z_halo():
+        for n, (side, index) in enumerate(((-1, 2), (1, 3))):
+            got = rcv.at[index]
+            for j, i in enumerate(dirs_where(2, side)):
+                z_cot[n, j, pl.ds(8, 8), :] = got[F_COT + j]
+            s = stress_of([got[F_CONF + k] for k in range(6)])
+            for a in range(3):
+                z_str[n, a] = s[slot[a, 2]]
+
+    def x_halo():
+        for side, index in ((-1, 0), (1, 1)):
+            rows = pl.ds(0 if side < 0 else 72, 8)
+            got = rcv.at[index]
+            p = [got[F_CONF + k] for k in range(6)]
+            s = stress_of(p)
+            for k in range(6):
+                x_conf[k, rows, :] = p[k]
+                x_str[k, rows, :] = s[k]
+            x_col[rows, :] = got[F_COL]
+            for j, i in enumerate(dirs_where(0, side)):
+                x_cot[i, rows, :] = got[F_COT + j]
+            for k in range(6):
+                (x_up if side < 0 else x_down)[k, rows, :] = got[F_UPW + k]
+        for n, side in enumerate((-1, 1)):
             for cx in (-1, 1):
-                if velocities[i][0] == cx:
-                    z_cot[n, j, pl.ds(7 if cx < 0 else 16, 1), :] = crcv[corners.index((cx, side)), pl.ds(C_OWN, 1), :]
-        s = stress_of([got[F_CONF + k] for k in range(6)])
-        for a in range(3):
-            z_str[n, a] = s[slot[a, 2]]
-
-    def halo_force(index):
+                j = dirs_where(2, side).index(corner_dir(cx, side))
+                row = crcv[corners.index((cx, side)), pl.ds(C_OWN, 1), :]
+                z_cot[n, j, pl.ds(7 if cx < 0 else 16, 1), :] = row
+
+    def halo_force(index, with_ends):
         axis, side = faces[index]
         across = 2 - axis
         edge = 0 if side < 0 else 7
@@ -386,14 +413,13 @@
 
         ends = {-1: first, 1: last}
         fills = {}
-        for end in (-1, 1):
+        for end in (-1, 1) if with_ends else ():
             c = corner_at(end)
             p = [crcv[c, pl.ds(C_CONF + k, 1), :] for k in range(6)]
             s = stress_of(p)
             fills[end] = ([s[slot[a, across]] for a in range(3)], crcv[c, pl.ds(C_COL, 1), :])
         c_halo = got[F_COL]
         mobility = 1.0 - c_halo * c_halo
-        low, high = fills[-1], fills[1]
 
         def at_ends(lo, hi):
             return jnp.where(first, rows_of(-0.5 * lo), jnp.where(last, rows_of(0.5 * hi), 0.0))
@@ -403,11 +429,13 @@
         c_edge = plane(v_col, axis, edge)
         force = []
         for a in range(3):
-            value = (-0.5 * side) * s[slot[a, axis]] + at_ends(low[0][a], high[0][a])
+            value = (-0.5 * side) * s[slot[a, axis]]
+            if with_ends:
+                value = value + at_ends(fills[-1][0][a], fills[1][0][a])
             if a == axis:
                 value = value + mobility * ((-0.5 * side) * c_edge)
-            elif a == across:
-                value = value + mobility * at_ends(low[1], high[1])
+            elif a == across and with_ends:
+                value = value + mobility * at_ends(fills[-1][1], fills[1][1])
             force.append(value)
         values = []
         for i in dirs_where(axis, -side):
@@ -419,11 +447,14 @@
                     n = 0 if end < 0 else 1
                     j = dirs_where(2, end).index(i)
                     row = z_cot[n, j, pl.ds(8 + edge, 1), :]
+                elif with_ends:
+                    row = x_cot[i, pl.ds((0 if end < 0 else 72) + edge, 1), :]
                 else:
-                    row = x_cot[i, pl.ds((0 if end < 0 else 72) + edge, 1), :]
-                value = shift(value, end, rows_of(row), rows_of(row))
+                    row = None
+                fill = None if row is None else rows_of(row)
+                value = shift(value, end, fill, fill)
             values.append((i, in_y(value, c[1])))
-        for end in (-1, 1):
+        for end in (-1, 1) if with_ends else ():
             c = corner_at(end)
             base = C_Z if axis == 0 else C_X
             for j, i in enumerate(edge_dirs(across, end, axis)):
@@ -441,8 +472,8 @@
         turned = apply(tensor, w)
         return [got[F_CHI] * (3.0 * one[a] + turned[a]) for a in range(3)]
 
-    for index in range(4):
-        h = halo_force(index)
+    def put_halo_force(index, with_ends):
+        h = halo_force(index, with_ends)
         for a in range(3):
             if index < 2:
                 x_h[a, pl.ds(0 if index == 0 else 72, 8), :] = h[a]
@@ -451,10 +482,10 @@
 
     def main(at, carry):
         def rows(by=0):
-            return pl.ds(pl.multiple_of(8 * (at + by), 8), 8)
+            return pl.ds(eights(at + by), 8)
 
         def padded(by=0):
-            return pl.ds(pl.multiple_of(8 * (at + by) + 8, 8), 8)
+            return pl.ds(eights(at + by + 1), 8)
 
         def z_row(ref, n, k):
             return rows_of(ref[n, k, pl.ds(at, 1), :])
@@ -547,14 +578,13 @@
             o_pop[i, rows(), :] = value
         return carry
 
-    lax.fori_loop(0, 8, main, 0)
 
     def finish(at, carry):
         def rows(by=0):
-            return pl.ds(pl.multiple_of(8 * (at + by), 8), 8)
+            return pl.ds(eights(at + by), 8)
 
         def padded(by=0):
-            return pl.ds(pl.multiple_of(8 * (at + by) + 8, 8), 8)
+            return pl.ds(eights(at + by + 1), 8)
 
         h = [x_h[a, padded(), :] for a in range(3)]
         u = [v_u[a, rows(), :] for a in range(3)]
@@ -625,7 +655,24 @@
             o_conf[k, rows(), :] = value
         return carry
 
-    lax.fori_loop(0, 8, finish, 0)
+    send_later((2, 3, 4, 5, 6, 7), False)
+    send_later((0, 1, 4, 5, 6, 7), True)
+    for k in (2, 3):
+        arrival[k].wait_recv()
+    z_halo()
+    put_halo_force(2, False)
+    put_halo_force(3, False)
+    lax.fori_loop(1, 7, main, 0)
+    lax.fori_loop(2, 6, finish, 0)
+    for k in (0, 1, 4, 5, 6, 7):
+        arrival[k].wait_recv()
+    x_halo()
+    for index in range(4):
+        put_halo_force(index, True)
+    for at in (0, 7):
+        main(at, 0)
+    for at in (0, 1, 6, 7):
+        finish(at, 0)
     for copy in copies:
         copy.wait_send()
 
@@ -654,7 +701,7 @@
     padded = [(19, 80, 128), (6, 80, 128), (80, 128), (6, 80, 128), (3, 80, 128), (6, 80, 128), (6, 80, 128)]
     scratch += [pltpu.VMEM(s, F32) for s in padded]
     scratch += [pltpu.VMEM(s, F32) for s in [(2, 5, 24, 128), (2, 3, 8, 128), (2, 3, 8, 128), (3, 64, 128), (64, 128)]]
-    scratch += [pltpu.SemaphoreType.DMA((6,))] + [pltpu.SemaphoreType.DMA((4,))] * 4
+    scratch += [pltpu.SemaphoreType.DMA((3, 6))] + [pltpu.SemaphoreType.DMA((4,))] * 4
     scratch += [pltpu.SemaphoreType.REGULAR((8,))]
     parts = pl.pallas_call(
         kernel,

time: 32.6 us -> 30 us (0.920)
  the two profiles are of different devices: /device:TPU:64 before, /device:TPU:128 now
where the time goes in v3:
time: 30 us; the launch traced here: 29.8 us
  Pallas kernels  29.2 us (97%)
  between operations  0.64 us (2%)
    pallas_call x1, Pallas kernels, body(): pl.pallas_call(kernel, out_shape=tuple((pltpu.VMEM(s, F32) for s in shape...  28.3 us
    pallas_call x1, Pallas kernels, body(): pl.pallas_call(deliver, out_shape=tuple((jax.ShapeDtypeStruct(s, F32) for...  0.92 us

profile of v3, /device:TPU:128, one launch (start us, length us, event | category | flops | bytes accessed | tf_op | source)
XLA Modules:
  0.0 29.8 jit_solution(4086297231598507376)
XLA Ops:
  0.6 28.3 %shard_map.85 = (f32[19,64,128]{2,1,0:T(8,128)S(1)}, f32[64,128]{1,0:T(8,128)S(1)}, f32[6,64,128]{2,1,0:T(8,128)S(1)}) custom-call(f32[19,64,128]{2,1,0:T(8,128)} %bitcast.9, f32[64,128]{1,0:T(8,128)} %bitcast.13, f32[6,64,128]{2,1,0:T(8,128)} %bitcast.11, s32[64,128]{1,0:T(8,128)} %bitcast.14, f32[19,64,128]{2,1,0:T(8,128)} %bitcast.10, f32[6,64,128]{2,1,0:T(8,128)} %bitcast.12), custom_call_target="tpu_custom_call" | custom-call | tf_op jit(solution)/shard_map/pallas_call | solution.py:706
  28.9 0.9 %shard_map.86 = (f32[19,64,128]{2,1,0:T(8,128)}, f32[64,128]{1,0:T(8,128)}, f32[6,64,128]{2,1,0:T(8,128)}) custom-call(f32[19,64,128]{2,1,0:T(8,128)S(1)} %get-tuple-element.9.a, f32[64,128]{1,0:T(8,128)S(1)} %get-tuple-element.10.b, f32[6,64,128]{2,1,0:T(8,128)S(1)} %get-tuple-element.11.c), custom_call_target="tpu_custom_call" | custom-call | tf_op jit(solution)/shard_map/pallas_call | solution.py:717

commit v4 on v3

--- a/solution.py
+++ b/solution.py
@@ -9,7 +9,7 @@
 
 MESH = pl.DeviceIdType.MESH
 F32 = jnp.float32
-LEVEL = (3, 6)
+LEVEL = (5, 6)
 
 velocities = (
     (0, 0, 0),
@@ -329,6 +329,8 @@
 
     for copy in outer:
         copy.wait()
+    for index in range(4):
+        make_corner(index)
     make_face(0)
     make_face(1)
     pl.semaphore_wait(barrier, expected)
@@ -338,14 +340,12 @@
         def _(k=k):
             pl.semaphore_signal(go_sem.at[flip[k]], inc=1, device_id=devices[k], device_id_type=MESH)
 
-    send((0, 1))
+    send((4, 5, 6, 7, 0, 1))
     for copy in middle:
         copy.wait()
-    for index in range(4):
-        make_corner(index)
     make_face(2)
     make_face(3)
-    send((4, 5, 6, 7, 3, 2))
+    send((3, 2))
 
     def local(at, carry):
         rows, padded = pl.ds(pl.multiple_of(8 * at, 8), 8), pl.ds(pl.multiple_of(8 * at + 8, 8), 8)
@@ -381,27 +381,25 @@
             for a in range(3):
                 z_str[n, a] = s[slot[a, 2]]
 
-    def x_halo():
-        for side, index in ((-1, 0), (1, 1)):
-            rows = pl.ds(0 if side < 0 else 72, 8)
-            got = rcv.at[index]
-            p = [got[F_CONF + k] for k in range(6)]
-            s = stress_of(p)
-            for k in range(6):
-                x_conf[k, rows, :] = p[k]
-                x_str[k, rows, :] = s[k]
-            x_col[rows, :] = got[F_COL]
-            for j, i in enumerate(dirs_where(0, side)):
-                x_cot[i, rows, :] = got[F_COT + j]
-            for k in range(6):
-                (x_up if side < 0 else x_down)[k, rows, :] = got[F_UPW + k]
-        for n, side in enumerate((-1, 1)):
-            for cx in (-1, 1):
-                j = dirs_where(2, side).index(corner_dir(cx, side))
-                row = crcv[corners.index((cx, side)), pl.ds(C_OWN, 1), :]
-                z_cot[n, j, pl.ds(7 if cx < 0 else 16, 1), :] = row
-
-    def halo_force(index, with_ends):
+    def x_halo(side):
+        index = 0 if side < 0 else 1
+        rows = pl.ds(0 if side < 0 else 72, 8)
+        got = rcv.at[index]
+        p = [got[F_CONF + k] for k in range(6)]
+        s = stress_of(p)
+        for k in range(6):
+            x_conf[k, rows, :] = p[k]
+            x_str[k, rows, :] = s[k]
+            (x_up if side < 0 else x_down)[k, rows, :] = got[F_UPW + k]
+        x_col[rows, :] = got[F_COL]
+        for j, i in enumerate(dirs_where(0, side)):
+            x_cot[i, rows, :] = got[F_COT + j]
+        for n, z_side in enumerate((-1, 1)):
+            j = dirs_where(2, z_side).index(corner_dir(side, z_side))
+            row = crcv[corners.index((side, z_side)), pl.ds(C_OWN, 1), :]
+            z_cot[n, j, pl.ds(7 if side < 0 else 16, 1), :] = row
+
+    def halo_force(index, given):
         axis, side = faces[index]
         across = 2 - axis
         edge = 0 if side < 0 else 7
@@ -413,7 +411,7 @@
 
         ends = {-1: first, 1: last}
         fills = {}
-        for end in (-1, 1) if with_ends else ():
+        for end in given:
             c = corner_at(end)
             p = [crcv[c, pl.ds(C_CONF + k, 1), :] for k in range(6)]
             s = stress_of(p)
@@ -421,8 +419,11 @@
         c_halo = got[F_COL]
         mobility = 1.0 - c_halo * c_halo
 
-        def at_ends(lo, hi):
-            return jnp.where(first, rows_of(-0.5 * lo), jnp.where(last, rows_of(0.5 * hi), 0.0))
+        def at_ends(pick):
+            value = 0.0
+            for end in given:
+                value = jnp.where(ends[end], rows_of((0.5 * end) * pick(fills[end])), value)
+            return value
 
         p = [plane(v_conf, axis, edge, k) for k in range(6)]
         s = stress_of(p)
@@ -430,12 +431,12 @@
         force = []
         for a in range(3):
             value = (-0.5 * side) * s[slot[a, axis]]
-            if with_ends:
-                value = value + at_ends(fills[-1][0][a], fills[1][0][a])
+            if given:
+                value = value + at_ends(lambda fill: fill[0][a])
             if a == axis:
                 value = value + mobility * ((-0.5 * side) * c_edge)
-            elif a == across and with_ends:
-                value = value + mobility * at_ends(fills[-1][1], fills[1][1])
+            elif a == across and given:
+                value = value + mobility * at_ends(lambda fill: fill[1])
             force.append(value)
         values = []
         for i in dirs_where(axis, -side):
@@ -447,14 +448,14 @@
                     n = 0 if end < 0 else 1
                     j = dirs_where(2, end).index(i)
                     row = z_cot[n, j, pl.ds(8 + edge, 1), :]
-                elif with_ends:
+                elif end in given:
                     row = x_cot[i, pl.ds((0 if end < 0 else 72) + edge, 1), :]
                 else:
                     row = None
                 fill = None if row is None else rows_of(row)
                 value = shift(value, end, fill, fill)
             values.append((i, in_y(value, c[1])))
-        for end in (-1, 1) if with_ends else ():
+        for end in given:
             c = corner_at(end)
             base = C_Z if axis == 0 else C_X
             for j, i in enumerate(edge_dirs(across, end, axis)):
@@ -472,8 +473,8 @@
         turned = apply(tensor, w)
         return [got[F_CHI] * (3.0 * one[a] + turned[a]) for a in range(3)]
 
-    def put_halo_force(index, with_ends):
-        h = halo_force(index, with_ends)
+    def put_halo_force(index, given):
+        h = halo_force(index, given)
         for a in range(3):
             if index < 2:
                 x_h[a, pl.ds(0 if index == 0 else 72, 8), :] = h[a]
@@ -655,24 +656,37 @@
             o_conf[k, rows(), :] = value
         return carry
 
-    send_later((2, 3, 4, 5, 6, 7), False)
+    send_later((4, 5, 6, 7, 2, 3), False)
     send_later((0, 1, 4, 5, 6, 7), True)
     for k in (2, 3):
         arrival[k].wait_recv()
     z_halo()
-    put_halo_force(2, False)
-    put_halo_force(3, False)
+    put_halo_force(2, ())
+    put_halo_force(3, ())
     lax.fori_loop(1, 7, main, 0)
     lax.fori_loop(2, 6, finish, 0)
-    for k in (0, 1, 4, 5, 6, 7):
-        arrival[k].wait_recv()
-    x_halo()
-    for index in range(4):
-        put_halo_force(index, True)
-    for at in (0, 7):
-        main(at, 0)
-    for at in (0, 1, 6, 7):
-        finish(at, 0)
+
+    def visit(turn, carry):
+        early = jnp.where(place == 0, 1, 0)
+        now = jnp.where(turn == 0, early, 1 - early)
+        for index, side in enumerate((-1, 1)):
+
+            @pl.when(now == index)
+            def _(index=index, side=side):
+                for k in (index, 4 + corners.index((side, -1)), 4 + corners.index((side, 1))):
+                    arrival[k].wait_recv()
+                x_halo(side)
+                put_halo_force(index, (-1, 1))
+                put_halo_force(2, (side,))
+                put_halo_force(3, (side,))
+                edge = 0 if side < 0 else 7
+                main(edge, 0)
+                finish(edge, 0)
+                finish(edge - side, 0)
+
+        return carry
+
+    lax.fori_loop(0, 2, visit, 0)
     for copy in copies:
         copy.wait_send()
 

time: 30 us -> 29.2 us (0.973)
  the two profiles are of different devices: /device:TPU:128 before, /device:TPU:32 now
where the time goes in v4:
time: 29.2 us; the launch traced here: 29.1 us
  Pallas kernels  28.5 us (98%)
  between operations  0.64 us (2%)
    pallas_call x1, Pallas kernels, body(): pl.pallas_call(kernel, out_shape=tuple((pltpu.VMEM(s, F32) for s in shape...  27.5 us
    pallas_call x1, Pallas kernels, body(): pl.pallas_call(deliver, out_shape=tuple((jax.ShapeDtypeStruct(s, F32) for...  0.92 us

profile of v4, /device:TPU:32, one launch (start us, length us, event | category | flops | bytes accessed | tf_op | source)
XLA Modules:
  0.0 29.1 jit_solution(12513727179870681733)
XLA Ops:
  0.6 27.5 %shard_map.85 = (f32[19,64,128]{2,1,0:T(8,128)S(1)}, f32[64,128]{1,0:T(8,128)S(1)}, f32[6,64,128]{2,1,0:T(8,128)S(1)}) custom-call(f32[19,64,128]{2,1,0:T(8,128)} %bitcast.9, f32[64,128]{1,0:T(8,128)} %bitcast.13, f32[6,64,128]{2,1,0:T(8,128)} %bitcast.11, s32[64,128]{1,0:T(8,128)} %bitcast.14, f32[19,64,128]{2,1,0:T(8,128)} %bitcast.10, f32[6,64,128]{2,1,0:T(8,128)} %bitcast.12), custom_call_target="tpu_custom_call" | custom-call | tf_op jit(solution)/shard_map/pallas_call | solution.py:720
  28.2 0.9 %shard_map.86 = (f32[19,64,128]{2,1,0:T(8,128)}, f32[64,128]{1,0:T(8,128)}, f32[6,64,128]{2,1,0:T(8,128)}) custom-call(f32[19,64,128]{2,1,0:T(8,128)S(1)} %get-tuple-element.9.a, f32[64,128]{1,0:T(8,128)S(1)} %get-tuple-element.10.b, f32[6,64,128]{2,1,0:T(8,128)S(1)} %get-tuple-element.11.c), custom_call_target="tpu_custom_call" | custom-call | tf_op jit(solution)/shard_map/pallas_call | solution.py:731

commit v5 on v4

--- a/solution.py
+++ b/solution.py
@@ -10,6 +10,7 @@
 MESH = pl.DeviceIdType.MESH
 F32 = jnp.float32
 LEVEL = (5, 6)
+DIRECT = 19
 
 velocities = (
     (0, 0, 0),
@@ -138,7 +139,7 @@
     v_pop, v_col, v_conf, v_lab, v_cot, v_con,
     snd, rcv, csnd, crcv,
     x_cot, x_conf, x_col, x_str, x_h, x_up, x_down, z_cot, z_str, z_h, v_u, v_ri,
-    in_sem, f_send, f_recv, c_send, c_recv, go_sem,
+    held, in_sem, f_send, f_recv, c_send, c_recv, go_sem, r_send, r_recv, h_send, h_recv, h_go,
 ):
     fields = [(conf, v_conf), (col, v_col), (cot, v_cot), (pop, v_pop), (lab, v_lab), (con, v_con)]
 
@@ -194,6 +195,38 @@
         def _(device=device):
             pl.semaphore_signal(barrier, inc=1, device_id=device, device_id_type=MESH)
 
+    def along(by):
+        return (z, lax.rem(x + by + nx, nx))
+
+    def relay_of(k):
+        return along(2 if k == 0 else -2)
+
+    def far_relay_of(k):
+        return along(-3 if k == 0 else 3)
+
+    serves = {0: place == 2, 1: place == 5}
+    owner = {0: along(-2), 1: along(2)}
+    target = {0: along(-3), 1: along(3)}
+    level_here = jnp.logical_and(z >= LEVEL[0], z <= LEVEL[1])
+    owner_follows = jnp.logical_and(upper == 0, jnp.logical_not(level_here))
+    owner_leads = jnp.logical_and(upper == 1, jnp.logical_not(level_here))
+    is_relay = jnp.logical_or(serves[0], serves[1])
+    expected = expected + jnp.where(jnp.logical_and(is_relay, jnp.logical_not(owner_follows)), 1, 0)
+    for k in (0, 1):
+        expected = expected + jnp.where(across_x[k], 1, 0) + jnp.where(leads[k], 1, 0)
+
+        @pl.when(jnp.logical_and(across_x[k], jnp.logical_not(leads[k])))
+        def _(k=k):
+            pl.semaphore_signal(barrier, inc=1, device_id=far_relay_of(k), device_id_type=MESH)
+
+        @pl.when(serves[k])
+        def _(k=k):
+            pl.semaphore_signal(barrier, inc=1, device_id=owner[k], device_id_type=MESH)
+
+        @pl.when(jnp.logical_and(serves[k], owner_follows))
+        def _(k=k):
+            pl.semaphore_signal(barrier, inc=1, device_id=target[k], device_id_type=MESH)
+
 
     lane = lax.broadcasted_iota(jnp.int32, (8, 128), 0)
     first, last = lane == 0, lane == 7
@@ -310,6 +343,71 @@
         for k in range(4)
     ]
     copies = face_copies + corner_copies
+    rest = F_ALL - DIRECT
+    direct = [
+        pltpu.make_async_remote_copy(
+            src_ref=snd.at[k, pl.ds(0, DIRECT)], dst_ref=rcv.at[k ^ 1, pl.ds(0, DIRECT)],
+            send_sem=f_send.at[k], recv_sem=f_recv.at[k ^ 1], device_id=face_device[k], device_id_type=MESH,
+        )
+        for k in (0, 1)
+    ]
+    to_relay = [
+        pltpu.make_async_remote_copy(
+            src_ref=snd.at[k, pl.ds(DIRECT, rest)], dst_ref=held, send_sem=r_send, recv_sem=r_recv,
+            device_id=relay_of(k), device_id_type=MESH,
+        )
+        for k in (0, 1)
+    ]
+    onwards = [
+        pltpu.make_async_remote_copy(
+            src_ref=held, dst_ref=rcv.at[k ^ 1, pl.ds(DIRECT, rest)], send_sem=h_send, recv_sem=h_recv,
+            device_id=target[k], device_id_type=MESH,
+        )
+        for k in (0, 1)
+    ]
+
+    def start(k):
+        if k > 1:
+            copies[k].start()
+            return
+
+        @pl.when(across_x[k])
+        def _():
+            direct[k].start()
+
+        @pl.when(jnp.logical_not(across_x[k]))
+        def _():
+            copies[k].start()
+
+    def wait_arrival(k):
+        if k > 1:
+            arrival[k].wait_recv()
+            return
+
+        @pl.when(across_x[k])
+        def _():
+            direct[flip[k]].wait_recv()
+            onwards[flip[k]].wait_recv()
+
+        @pl.when(jnp.logical_not(across_x[k]))
+        def _():
+            arrival[k].wait_recv()
+
+    def relay(when):
+        for k in (0, 1):
+
+            @pl.when(jnp.logical_and(serves[k], when))
+            def _(k=k):
+                to_relay[k].wait_recv()
+
+        for k in (0, 1):
+
+            @pl.when(jnp.logical_and(serves[k], when))
+            def _(k=k):
+                if when is owner_follows:
+                    pl.semaphore_wait(h_go, 1)
+                onwards[k].start()
+
     arrival = [copies[k] for k in flip]
 
     def send(ks):
@@ -317,7 +415,7 @@
 
             @pl.when(jnp.logical_not(follows[k]))
             def _(k=k):
-                copies[k].start()
+                start(k)
 
     def send_later(ks, over_x):
         for k in ks:
@@ -325,7 +423,7 @@
             @pl.when(jnp.logical_and(follows[k], jnp.equal(across_x[k], over_x)))
             def _(k=k):
                 pl.semaphore_wait(go_sem.at[k], 1)
-                copies[k].start()
+                start(k)
 
     for copy in outer:
         copy.wait()
@@ -340,7 +438,18 @@
         def _(k=k):
             pl.semaphore_signal(go_sem.at[flip[k]], inc=1, device_id=devices[k], device_id_type=MESH)
 
+    for k in (0, 1):
+
+        @pl.when(leads[k])
+        def _(k=k):
+            pl.semaphore_signal(h_go, inc=1, device_id=far_relay_of(k), device_id_type=MESH)
+
+        @pl.when(across_x[k])
+        def _(k=k):
+            to_relay[k].start()
+
     send((4, 5, 6, 7, 0, 1))
+    relay(jnp.logical_not(owner_follows))
     for copy in middle:
         copy.wait()
     make_face(2)
@@ -658,8 +767,9 @@
 
     send_later((4, 5, 6, 7, 2, 3), False)
     send_later((0, 1, 4, 5, 6, 7), True)
+    relay(owner_follows)
     for k in (2, 3):
-        arrival[k].wait_recv()
+        wait_arrival(k)
     z_halo()
     put_halo_force(2, ())
     put_halo_force(3, ())
@@ -674,7 +784,7 @@
             @pl.when(now == index)
             def _(index=index, side=side):
                 for k in (index, 4 + corners.index((side, -1)), 4 + corners.index((side, 1))):
-                    arrival[k].wait_recv()
+                    wait_arrival(k)
                 x_halo(side)
                 put_halo_force(index, (-1, 1))
                 put_halo_force(2, (side,))
@@ -687,8 +797,22 @@
         return carry
 
     lax.fori_loop(0, 2, visit, 0)
-    for copy in copies:
+    for copy in copies[2:]:
         copy.wait_send()
+    for k in (0, 1):
+
+        @pl.when(across_x[k])
+        def _(k=k):
+            direct[k].wait_send()
+            to_relay[k].wait_send()
+
+        @pl.when(jnp.logical_not(across_x[k]))
+        def _(k=k):
+            copies[k].wait_send()
+
+        @pl.when(serves[k])
+        def _(k=k):
+            onwards[k].wait_send()
 
 
 def deliver(a, b, c, out_a, out_b, out_c, sem):
@@ -715,8 +839,10 @@
     padded = [(19, 80, 128), (6, 80, 128), (80, 128), (6, 80, 128), (3, 80, 128), (6, 80, 128), (6, 80, 128)]
     scratch += [pltpu.VMEM(s, F32) for s in padded]
     scratch += [pltpu.VMEM(s, F32) for s in [(2, 5, 24, 128), (2, 3, 8, 128), (2, 3, 8, 128), (3, 64, 128), (64, 128)]]
+    scratch += [pltpu.VMEM((F_ALL - DIRECT, 8, 128), F32)]
     scratch += [pltpu.SemaphoreType.DMA((3, 6))] + [pltpu.SemaphoreType.DMA((4,))] * 4
     scratch += [pltpu.SemaphoreType.REGULAR((8,))]
+    scratch += [pltpu.SemaphoreType.DMA] * 4 + [pltpu.SemaphoreType.REGULAR]
     parts = pl.pallas_call(
         kernel,
         out_shape=tuple(pltpu.VMEM(s, F32) for s in shapes),

time: 29.2 us -> 27.1 us (0.928)
  the two profiles are of different devices: /device:TPU:32 before, /device:TPU:408 now
where the time goes in v5:
time: 27.1 us; the launch traced here: 27 us
  Pallas kernels  26.3 us (97%)
  between operations  0.64 us (2%)
    pallas_call x1, Pallas kernels, body(): pl.pallas_call(kernel, out_shape=tuple((pltpu.VMEM(s, F32) for s in shape...  25.4 us
    pallas_call x1, Pallas kernels, body(): pl.pallas_call(deliver, out_shape=tuple((jax.ShapeDtypeStruct(s, F32) for...  0.92 us

profile of v5, /device:TPU:408, one launch (start us, length us, event | category | flops | bytes accessed | tf_op | source)
XLA Modules:
  0.0 27.0 jit_solution(16519727539918975539)
XLA Ops:
  0.6 25.4 %shard_map.85 = (f32[19,64,128]{2,1,0:T(8,128)S(1)}, f32[64,128]{1,0:T(8,128)S(1)}, f32[6,64,128]{2,1,0:T(8,128)S(1)}) custom-call(f32[19,64,128]{2,1,0:T(8,128)} %bitcast.9, f32[64,128]{1,0:T(8,128)} %bitcast.13, f32[6,64,128]{2,1,0:T(8,128)} %bitcast.11, s32[64,128]{1,0:T(8,128)} %bitcast.14, f32[19,64,128]{2,1,0:T(8,128)} %bitcast.10, f32[6,64,128]{2,1,0:T(8,128)} %bitcast.12), custom_call_target="tpu_custom_call" | custom-call | tf_op jit(solution)/shard_map/pallas_call | solution.py:846
  26.0 0.9 %shard_map.86 = (f32[19,64,128]{2,1,0:T(8,128)}, f32[64,128]{1,0:T(8,128)}, f32[6,64,128]{2,1,0:T(8,128)}) custom-call(f32[19,64,128]{2,1,0:T(8,128)S(1)} %get-tuple-element.9.a, f32[64,128]{1,0:T(8,128)S(1)} %get-tuple-element.10.b, f32[6,64,128]{2,1,0:T(8,128)S(1)} %get-tuple-element.11.c), custom_call_target="tpu_custom_call" | custom-call | tf_op jit(solution)/shard_map/pallas_call | solution.py:857

commit v6 on v5

--- a/solution.py
+++ b/solution.py
@@ -9,8 +9,8 @@
 
 MESH = pl.DeviceIdType.MESH
 F32 = jnp.float32
-LEVEL = (5, 6)
-DIRECT = 19
+MID = (4, 6)
+DIRECT = 21
 
 velocities = (
     (0, 0, 0),
@@ -176,11 +176,9 @@
     follows, leads, across_x = [], [], []
     for dx, dz in offsets:
         far_x, far_z = edge_x[dx], edge_z[dz]
-        level = jnp.logical_and(jnp.minimum(z, z + dz) >= LEVEL[0], jnp.maximum(z, z + dz) <= LEVEL[1])
-        far_x_led = jnp.logical_and(far_x, jnp.logical_not(level))
-        far = jnp.logical_or(far_x_led, far_z)
+        far = jnp.logical_or(far_x, far_z)
         follow = jnp.logical_or(
-            jnp.logical_and(far_x_led, upper == 0),
+            jnp.logical_and(far_x, upper == 0),
             jnp.logical_and(jnp.logical_and(far_z, jnp.logical_not(far_x)), z == 0),
         )
         follows.append(follow)
@@ -207,26 +205,31 @@
     serves = {0: place == 2, 1: place == 5}
     owner = {0: along(-2), 1: along(2)}
     target = {0: along(-3), 1: along(3)}
-    level_here = jnp.logical_and(z >= LEVEL[0], z <= LEVEL[1])
-    owner_follows = jnp.logical_and(upper == 0, jnp.logical_not(level_here))
-    owner_leads = jnp.logical_and(upper == 1, jnp.logical_not(level_here))
-    is_relay = jnp.logical_or(serves[0], serves[1])
-    expected = expected + jnp.where(jnp.logical_and(is_relay, jnp.logical_not(owner_follows)), 1, 0)
+    owner_follows = upper == 0
+    mid = jnp.logical_and(z >= MID[0], z <= MID[1])
+    early_relay = jnp.logical_or(jnp.logical_not(owner_follows), mid)
+    late_relay = jnp.logical_not(early_relay)
+    heard = jnp.where(owner_follows, jnp.where(mid, 2, 0), 1)
+    expected = expected + jnp.where(jnp.logical_or(serves[0], serves[1]), heard, 0)
+    led_far = [jnp.logical_and(leads[k], jnp.logical_not(mid)) for k in (0, 1)]
     for k in (0, 1):
-        expected = expected + jnp.where(across_x[k], 1, 0) + jnp.where(leads[k], 1, 0)
-
-        @pl.when(jnp.logical_and(across_x[k], jnp.logical_not(leads[k])))
+        expected = expected + jnp.where(across_x[k], 1, 0) + jnp.where(led_far[k], 1, 0)
+
+        @pl.when(jnp.logical_and(across_x[k], jnp.logical_not(led_far[k])))
         def _(k=k):
             pl.semaphore_signal(barrier, inc=1, device_id=far_relay_of(k), device_id_type=MESH)
 
+        @pl.when(jnp.logical_and(follows[k], mid))
+        def _(k=k):
+            pl.semaphore_signal(barrier, inc=1, device_id=relay_of(k), device_id_type=MESH)
+
         @pl.when(serves[k])
         def _(k=k):
             pl.semaphore_signal(barrier, inc=1, device_id=owner[k], device_id_type=MESH)
 
-        @pl.when(jnp.logical_and(serves[k], owner_follows))
+        @pl.when(jnp.logical_and(serves[k], late_relay))
         def _(k=k):
             pl.semaphore_signal(barrier, inc=1, device_id=target[k], device_id_type=MESH)
-
 
     lane = lax.broadcasted_iota(jnp.int32, (8, 128), 0)
     first, last = lane == 0, lane == 7
@@ -404,7 +407,7 @@
 
             @pl.when(jnp.logical_and(serves[k], when))
             def _(k=k):
-                if when is owner_follows:
+                if when is late_relay:
                     pl.semaphore_wait(h_go, 1)
                 onwards[k].start()
 
@@ -434,13 +437,17 @@
     pl.semaphore_wait(barrier, expected)
     for k in range(8):
 
-        @pl.when(leads[k])
+        @pl.when(leads[k] if k > 1 else led_far[k])
         def _(k=k):
             pl.semaphore_signal(go_sem.at[flip[k]], inc=1, device_id=devices[k], device_id_type=MESH)
 
     for k in (0, 1):
 
-        @pl.when(leads[k])
+        @pl.when(jnp.logical_and(serves[k], jnp.logical_and(owner_follows, mid)))
+        def _(k=k):
+            pl.semaphore_signal(go_sem.at[k], inc=1, device_id=owner[k], device_id_type=MESH)
+
+        @pl.when(led_far[k])
         def _(k=k):
             pl.semaphore_signal(h_go, inc=1, device_id=far_relay_of(k), device_id_type=MESH)
 
@@ -449,7 +456,7 @@
             to_relay[k].start()
 
     send((4, 5, 6, 7, 0, 1))
-    relay(jnp.logical_not(owner_follows))
+    relay(early_relay)
     for copy in middle:
         copy.wait()
     make_face(2)
@@ -767,7 +774,7 @@
 
     send_later((4, 5, 6, 7, 2, 3), False)
     send_later((0, 1, 4, 5, 6, 7), True)
-    relay(owner_follows)
+    relay(late_relay)
     for k in (2, 3):
         wait_arrival(k)
     z_halo()

time: 27.1 us -> 26.7 us (0.985)
  the two profiles are of different devices: /device:TPU:408 before, /device:TPU:32 now
where the time goes in v6:
time: 26.7 us; the launch traced here: 26.6 us
  Pallas kernels  25.9 us (97%)
  between operations  0.64 us (2%)
    pallas_call x1, Pallas kernels, body(): pl.pallas_call(kernel, out_shape=tuple((pltpu.VMEM(s, F32) for s in shape...  25 us
    pallas_call x1, Pallas kernels, body(): pl.pallas_call(deliver, out_shape=tuple((jax.ShapeDtypeStruct(s, F32) for...  0.92 us

profile of v6, /device:TPU:32, one launch (start us, length us, event | category | flops | bytes accessed | tf_op | source)
XLA Modules:
  0.0 26.6 jit_solution(10738209322799418778)
XLA Ops:
  0.6 25.0 %shard_map.85 = (f32[19,64,128]{2,1,0:T(8,128)S(1)}, f32[64,128]{1,0:T(8,128)S(1)}, f32[6,64,128]{2,1,0:T(8,128)S(1)}) custom-call(f32[19,64,128]{2,1,0:T(8,128)} %bitcast.9, f32[64,128]{1,0:T(8,128)} %bitcast.13, f32[6,64,128]{2,1,0:T(8,128)} %bitcast.11, s32[64,128]{1,0:T(8,128)} %bitcast.14, f32[19,64,128]{2,1,0:T(8,128)} %bitcast.10, f32[6,64,128]{2,1,0:T(8,128)} %bitcast.12), custom_call_target="tpu_custom_call" | custom-call | tf_op jit(solution)/shard_map/pallas_call | solution.py:853
  25.7 0.9 %shard_map.86 = (f32[19,64,128]{2,1,0:T(8,128)}, f32[64,128]{1,0:T(8,128)}, f32[6,64,128]{2,1,0:T(8,128)}) custom-call(f32[19,64,128]{2,1,0:T(8,128)S(1)} %get-tuple-element.9.a, f32[64,128]{1,0:T(8,128)S(1)} %get-tuple-element.10.b, f32[6,64,128]{2,1,0:T(8,128)S(1)} %get-tuple-element.11.c), custom_call_target="tpu_custom_call" | custom-call | tf_op jit(solution)/shard_map/pallas_call | solution.py:864

commit v7 on v6

--- a/solution.py
+++ b/solution.py
@@ -840,7 +840,7 @@
         for v in (populations, colour, conformation, labels, pop_cotangent, conf_cotangent)
     ]
     shapes = [(19, 64, 128), (64, 128), (6, 64, 128)]
-    scratch = [pltpu.VMEM(v.shape, v.dtype) for v in args]
+    scratch = [pltpu.VMEM(v.shape[:-2] + (72, 128), v.dtype) for v in args]
     scratch += [pltpu.VMEM((4, F_ALL, 8, 128), F32)] * 2
     scratch += [pltpu.VMEM((4, C_ALL, 128), F32)] * 2
     padded = [(19, 80, 128), (6, 80, 128), (80, 128), (6, 80, 128), (3, 80, 128), (6, 80, 128), (6, 80, 128)]

time: 26.7 us -> 26.7 us (level)
  no operation moved by 1% of the time
where the time goes in v7:
time: 26.7 us; the launch traced here: 26.6 us
  Pallas kernels  25.9 us (97%)
  between operations  0.64 us (2%)
    pallas_call x1, Pallas kernels, body(): pl.pallas_call(kernel, out_shape=tuple((pltpu.VMEM(s, F32) for s in shape...  25 us
    pallas_call x1, Pallas kernels, body(): pl.pallas_call(deliver, out_shape=tuple((jax.ShapeDtypeStruct(s, F32) for...  0.92 us

profile of v7, /device:TPU:32, one launch (start us, length us, event | category | flops | bytes accessed | tf_op | source)
XLA Modules:
  0.0 26.6 jit_solution(4783746565192552091)
XLA Ops:
  0.6 25.0 %shard_map.85 = (f32[19,64,128]{2,1,0:T(8,128)S(1)}, f32[64,128]{1,0:T(8,128)S(1)}, f32[6,64,128]{2,1,0:T(8,128)S(1)}) custom-call(f32[19,64,128]{2,1,0:T(8,128)} %bitcast.9, f32[64,128]{1,0:T(8,128)} %bitcast.13, f32[6,64,128]{2,1,0:T(8,128)} %bitcast.11, s32[64,128]{1,0:T(8,128)} %bitcast.14, f32[19,64,128]{2,1,0:T(8,128)} %bitcast.10, f32[6,64,128]{2,1,0:T(8,128)} %bitcast.12), custom_call_target="tpu_custom_call" | custom-call | tf_op jit(solution)/shard_map/pallas_call | solution.py:853
  25.7 0.9 %shard_map.86 = (f32[19,64,128]{2,1,0:T(8,128)}, f32[64,128]{1,0:T(8,128)}, f32[6,64,128]{2,1,0:T(8,128)}) custom-call(f32[19,64,128]{2,1,0:T(8,128)S(1)} %get-tuple-element.9.a, f32[64,128]{1,0:T(8,128)S(1)} %get-tuple-element.10.b, f32[6,64,128]{2,1,0:T(8,128)S(1)} %get-tuple-element.11.c), custom_call_target="tpu_custom_call" | custom-call | tf_op jit(solution)/shard_map/pallas_call | solution.py:864
